TPU v7x, 512 devices: a whole 4x8x8 slice. The times are simulated.
512 devices in a mesh: dp: 8 (over y), fsdp: 64 (over x, z, core).
Axes of the slice: x: 4, y: 8, z: 8, core: 2. Of those that a mesh axis runs over, the one named last changes fastest.
Arguments:
- gradients: bfloat16 [8, 256, 512, 512], P('dp', None, 'fsdp')
- statistics: float32 [512, 512, 512], P(('dp', 'fsdp')), as said below
- newton_steps: int32 [512], P(('dp', 'fsdp')), may hold values from 1 to 3, as said below
- second_moment: float32 [256, 512, 512], P('dp', 'fsdp'), may hold values from 0.01 to 1
Outputs:
- update: bfloat16 [256, 512, 512], P('dp', 'fsdp')
- new_moment: float32 [256, 512, 512], P('dp', 'fsdp')
Inputs may be any that keep to these rules, and one draw needn't show every extreme that they name: `newton_steps`: each factor takes 1, 2 or 3 iterations; about half take one; some factor takes 3 and some takes 1 in every draw. `statistics`: each matrix is symmetric with a positive diagonal and strictly dominant diagonal after symmetric scaling.
All inputs are finite; a program needn't handle non-finite values.
Results may differ from a plain program's by a relative error of at most 0.002.
The roundings to bfloat16 on the way count: a program that leaves them out, or rounds other values in their place, can miss the bound.
Values may be sent and summed in bfloat16 or wider, within the bound.
A program may use at most 64 MiB of HBM per device.

v0:
```python
import jax
import jax.numpy as jnp
from jax import lax
from jax.sharding import PartitionSpec as P

stat_decay = 0.9
moment_decay = 0.95
adam_eps = 1e-08
ratio_eps = 1e-06
HIGH = lax.Precision.HIGHEST


def from_partner(value, axis, stride):
    mask = 2**stride
    pairs = [(source, source ^ mask) for source in range(lax.axis_size(axis))]
    return lax.ppermute(value, axis, pairs)


def inverse_root(statistic, step_count):
    identity = jnp.eye(statistic.shape[0], dtype=jnp.float32)
    frobenius = jnp.sqrt(jnp.sum(statistic * statistic))
    scaling = 5.0 / (2.0 * frobenius)
    start = (jnp.sqrt(jnp.sqrt(scaling)) * identity, scaling * statistic)

    def one_step(counter, state_pair):
        iterate, moment_m = state_pair
        factor = (5.0 * identity - moment_m) / 4.0
        iterate = jnp.dot(iterate, factor, precision=HIGH)
        square = jnp.dot(factor, factor, precision=HIGH)
        fourth = jnp.dot(square, square, precision=HIGH)
        moment_m = jnp.dot(fourth, moment_m, precision=HIGH)
        return (iterate, moment_m)

    iterate, moment_m = lax.fori_loop(0, step_count, one_step, start)
    return iterate.astype(jnp.bfloat16)


def on_device(gradients, statistics, newton_steps, second_moment):
    replica_count = lax.axis_size("dp")
    owner_count = lax.axis_size("fsdp")
    summed = lax.psum_scatter(
        gradients[0].astype(jnp.float32), "dp", scatter_dimension=0, tiled=True
    )
    grad_mean = summed / replica_count
    grad_bf = grad_mean.astype(jnp.bfloat16)
    blocks_here, row_count, width = grad_bf.shape
    half_width = width // 2
    side_index = lax.axis_index("fsdp") % 2
    doubled = jnp.broadcast_to(grad_bf[:, None], (blocks_here, 2, row_count, width))
    doubled = doubled.reshape(2 * blocks_here, row_count, width)
    owned = lax.all_to_all(doubled, "fsdp", split_axis=0, concat_axis=1, tiled=True)[0]
    chosen = jnp.where(side_index == 0, owned, owned.T)
    gram = jnp.dot(chosen, chosen.T, preferred_element_type=jnp.float32)
    statistic = stat_decay * statistics[0] + (1.0 - stat_decay) * gram
    root = inverse_root(statistic, newton_steps[0])
    partner_root = from_partner(root, "fsdp", 0)
    left_root = jnp.where(side_index == 0, root, partner_root)
    right_root = jnp.where(side_index == 0, partner_root, root)
    middle = jnp.dot(left_root, owned, preferred_element_type=jnp.float32).astype(jnp.bfloat16)
    right_cols = lax.dynamic_slice_in_dim(right_root, side_index * half_width, half_width, 1)
    dir_half = jnp.dot(middle, right_cols, preferred_element_type=jnp.float32).astype(jnp.bfloat16)
    pieces = dir_half.reshape(owner_count, row_count, half_width)
    returned = lax.all_to_all(pieces, "fsdp", split_axis=0, concat_axis=0, tiled=True)
    direction = returned.reshape(blocks_here, 2, row_count, half_width).transpose(0, 2, 1, 3)
    direction = direction.reshape(blocks_here, row_count, width)
    new_moment = moment_decay * second_moment + (1.0 - moment_decay) * grad_mean * grad_mean
    adam = grad_mean / (jnp.sqrt(new_moment) + adam_eps)
    dir_wide = direction.astype(jnp.float32)
    adam_part = jnp.sum(adam * adam, axis=(1, 2))
    dir_part = jnp.sum(dir_wide * dir_wide, axis=(1, 2))
    adam_sq, dir_sq = lax.psum((adam_part, dir_part), "fsdp")
    ratio = jnp.sqrt(adam_sq) / (jnp.sqrt(dir_sq) + ratio_eps)
    update = (dir_wide * ratio[:, None, None]).astype(jnp.bfloat16)
    return (update, new_moment)


def solution(mesh):
    return jax.shard_map(
        on_device,
        mesh=mesh,
        in_specs=(
            P("dp", None, "fsdp", None),
            P(("dp", "fsdp"), None, None),
            P(("dp", "fsdp")),
            P("dp", "fsdp", None),
        ),
        out_specs=(P("dp", "fsdp", None), P("dp", "fsdp", None)),
        check_vma=False,
    )
```

profile of v0, /device:TPU:1, one launch (start us, length us, event | category | flops | bytes accessed | tf_op | source)
XLA Modules:
  0.0 288.2 jit_solution(10256711148539268038)
XLA Ops:
  7.2 0.0 copy-start
  7.2 0.0 reduce-scatter.2.cloned.1.call-start
  7.2 4.2 %bitcast_convert_fusion = f32[256,8,512]{2,1,0:T(8,128)} fusion(bf16[1,256,8,512]{3,2,1,0:T(8,128)(2,1)} %param.6), kind=kLoop, calls=%fused_computation.18 | loop fusion | flops 1048576 | bytes 6291456 | tf_op jit(solution)/shard_map/convert_element_type | solution.py:42
  11.4 0.0 copy-start.1
  11.4 0.0 reduce-scatter.2.cloned.1.call-update
  11.4 63.3 %reduce-scatter.2.cloned.1.call-done = f32[32,8,512]{2,1,0:T(8,128)} async-done(((f32[256,8,512]{2,1,0:T(8,128)}), f32[32,8,512]{2,1,0:T(8,128)}) %reduce-scatter.2.cloned.1.call-update) | async-done | bytes 524304 | tf_op jit(solution)/shard_map/reduce_scatter | solution.py:41
  74.7 0.0 copy-done
  74.7 2.2 multiply_reduce_fusion.2
  76.9 0.8 broadcast_in_dim.2
  77.7 11.0 %all-to-all-start = ((bf16[64,8,512]{2,1,0:T(8,128)(2,1)}), bf16[64,8,512]{2,1,0:T(8,128)(2,1)S(1)}, u32[]{:S(2)}, u32[]{:S(2)}) async-start(bf16[64,8,512]{2,1,0:T(8,128)(2,1)} %bitcast.2), calls=%async_computation.1 | async-start | bytes 1048576 | tf_op jit(solution)/shard_map/all_to_all | solution.py:51
  88.7 17.3 %all-to-all-done = bf16[64,8,512]{2,1,0:T(8,128)(2,1)S(1)} async-done(((bf16[64,8,512]{2,1,0:T(8,128)(2,1)}), bf16[64,8,512]{2,1,0:T(8,128)(2,1)S(1)}, u32[]{:S(2)}, u32[]{:S(2)}) %all-to-all-start) | async-done | bytes 524320 | tf_op jit(solution)/shard_map/all_to_all | solution.py:51
  106.0 0.2 copy.7
  106.2 0.0 copy-done.1
  106.3 1.3 multiply_reduce_fusion
  108.4 0.1 broadcast_multiply_fusion
  108.5 0.1 fusion.22
  108.7 9.0 %while.13 = (s32[]{:T(128)}, f32[512,512]{0,1:T(8,128)S(1)}, f32[512,512]{1,0:T(8,128)S(1)}, s32[]{:T(128)}, s32[]{:T(128)}) while((s32[]{:T(128)}, f32[512,512]{0,1:T(8,128)S(1)}, f32[512,512]{1,0:T(8,128)S(1)}, s32[]{:T(128)}, s32[]{:T(128)}) %tuple.28), condition=%wide.region_3.4_spmd.clone, body=%wide.region_2.3_spmd.clone.sunk | while | flops 6444548096 | bytes 14680125 | solution.py:34
  109.3 0.1 copy.19
  109.4 0.1 copy.20
  109.5 1.9 fusion.57
  111.4 1.8 fusion.58
  113.3 1.9 convolution_bitcast_fusion.2
  115.2 1.9 fusion.59
  117.7 0.1 convert_element_type.45
  117.8 10.6 %collective-permute-start = (bf16[512,512]{0,1:T(8,128)(2,1)S(1)}, bf16[512,512]{0,1:T(8,128)(2,1)S(1)}, u32[]{:S(2)}, u32[]{:S(2)}) collective-permute-start(bf16[512,512]{0,1:T(8,128)(2,1)S(1)} %convert_element_type.45), channel_id=1, source_target_pairs={{0,1},{1,0},{2,3},{3,2},{4,5},{5,4},{6,7},{7,6},{8,9},{9,8},{10,11... | collective-permute-start | bytes 1572872 | tf_op jit(solution)/shard_map/ppermute | solution.py:16
  128.4 1.5 collective-permute-done
  129.9 0.7 fusion.21
  130.6 25.2 %all_to_all.14 = bf16[64,8,256]{2,1,0:T(8,128)(2,1)S(1)} all-to-all(bf16[64,8,256]{2,1,0:T(8,128)(2,1)S(1)} %fusion.21), channel_id=1, replica_groups=mesh['dp'=8,'fsdp'=64] {'fsdp'}, dimensions={0} | all-to-all | bytes 524288 | tf_op jit(solution)/shard_map/all_to_all | solution.py:63
  155.8 0.6 multiply_reduce_fusion.1
  156.4 0.1 reduce_sum.37
  156.5 0.1 reduce_sum.38
  156.6 123.9 %all-reduce = (f32[32]{0:T(128)S(1)}, f32[32]{0:T(128)S(1)}) all-reduce(f32[32]{0:T(128)S(1)} %reduce_sum.38, f32[32]{0:T(128)S(1)} %get-tuple-element.52), channel_id=1, replica_groups=mesh['dp'=8,'fsdp'=64] {'fsdp'}, use_global_device_ids=true, to_apply=%region_8.9 | all-reduce | flops 64 | bytes 512 | tf_op jit(solution)/shard_map/psum | solution.py:71
  280.5 0.8 multiply_convert_fusion
  (2 shorter events, 0.1 us)
Async XLA Ops:
  7.2 67.5 %copy-start = (f32[32,8,512]{2,1,0:T(8,128)S(1)}, f32[32,8,512]{2,1,0:T(8,128)}, u32[]{:S(2)}) copy-start(f32[32,8,512]{2,1,0:T(8,128)} %param.9) | copy-start | bytes 1572868
  7.2 67.5 %reduce-scatter.2.cloned.1.call-start = ((), (), s32[]{:S(2)}) async-start(), calls=%async_computation.3 | async-start | bytes 4718592 | tf_op jit(solution)/shard_map/reduce_scatter | solution.py:41
  11.4 94.9 %copy-start.1 = (f32[1,512,512]{2,1,0:T(8,128)S(1)}, f32[1,512,512]{2,1,0:T(8,128)}, u32[]{:S(2)}) copy-start(f32[1,512,512]{2,1,0:T(8,128)} %param.7) | copy-start | bytes 3145732
  77.7 28.3 %all-to-all-start = ((bf16[64,8,512]{2,1,0:T(8,128)(2,1)}), bf16[64,8,512]{2,1,0:T(8,128)(2,1)S(1)}, u32[]{:S(2)}, u32[]{:S(2)}) async-start(bf16[64,8,512]{2,1,0:T(8,128)(2,1)} %bitcast.2), calls=%async_computation.1 | async-start | bytes 1048576 | tf_op jit(solution)/shard_map/all_to_all | solution.py:51
  117.8 12.1 %collective-permute-start = (bf16[512,512]{0,1:T(8,128)(2,1)S(1)}, bf16[512,512]{0,1:T(8,128)(2,1)S(1)}, u32[]{:S(2)}, u32[]{:S(2)}) collective-permute-start(bf16[512,512]{0,1:T(8,128)(2,1)S(1)} %convert_element_type.45), channel_id=1, source_target_pairs={{0,1},{1,0},{2,3},{3,2},{4,5},{5,4},{6,7},{7,6},{8,9},{9,8},{10,11... | collective-permute-start | bytes 1572872 | tf_op jit(solution)/shard_map/ppermute | solution.py:16
Sparse Core Ops, SparseCore 0:
  11.5 63.1 reduce-scatter.1
where the time goes:
time: 290 us; the launch traced here: 288 us
  blocking collectives  149 us (51%)
  waiting for transfers between devices  82.1 us (28%)
  starting transfers between devices  21.6 us (7%)
  between operations  15 us (5%)
  matrix products  9.55 us (3%)
  other arithmetic  8.15 us (3%)
    psum x1, blocking collectives, on_device(): adam_sq, dir_sq = lax.psum((adam_part, dir_part), 'fsdp')  124 us
    reduce_scatter x1, waiting for transfers between devices, on_device(): lax.psum_scatter(gradients[0].astype(jnp.float32), 'dp', scatter_dimensio...  63.3 us
    all_to_all x1, blocking collectives, on_device(): lax.all_to_all(pieces, 'fsdp', split_axis=0, concat_axis=0, tiled=True)  25.2 us
    all_to_all x1, waiting for transfers between devices, on_device(): lax.all_to_all(doubled, 'fsdp', split_axis=0, concat_axis=1, tiled=True)[0]  17.3 us
    all_to_all x1, starting transfers between devices, on_device(): lax.all_to_all(doubled, 'fsdp', split_axis=0, concat_axis=1, tiled=True)[0]  11 us
    ppermute x1, starting transfers between devices, from_partner(): return lax.ppermute(value, axis, pairs)  10.6 us
  transfers between devices with their start and end apart: 3, of which 3 were waited for; matrix products, arithmetic and copies ran while one was open for 0% of the time, Pallas kernels for 0%

commit v1 on v0

v1 whole, which is shorter than its diff:
```python
import functools

import jax
import jax.numpy as jnp
from jax import lax
from jax.experimental import pallas as pl
from jax.experimental.pallas import tpu as pltpu
from jax.sharding import PartitionSpec as P

stat_decay = 0.9
moment_decay = 0.95
adam_eps = 1e-08
ratio_eps = 1e-06
MESH = pl.DeviceIdType.MESH
F32 = jnp.float32
BF16 = jnp.bfloat16
LANES = 128
ROWS = 8
TILE = 64
SIZE = 512
WAYS = 8
COLS = 4
RINGS = 8
OWNERS = 64
HALF = OWNERS // 2
MSG = 48


def kernel(
    grad, stats, steps, second, upd, moment,
    own, stat_v, second_v, moment_v,
    r1, leaf, r2, s2, s3, r3, r4,
    outgoing, gathered, block, middle, direction, back, roots,
    a_f, p_f, q_f, r_f, m_f, x_f,
    a_l, b_l, m_l, x_l, t_r, u_r,
    local_sem, ring_send, ring_recv, row_send, row_recv, root_send, root_recv, back_send, back_recv,
):
    y = lax.axis_index("dp")
    me = lax.axis_index("fsdp")
    core = lax.rem(me, 2)
    chip = lax.div(me, 2)
    z = lax.rem(chip, RINGS)

    own_copy = pltpu.make_async_copy(grad, own, local_sem.at[0])
    stat_copy = pltpu.make_async_copy(stats, stat_v, local_sem.at[1])
    second_copy = pltpu.make_async_copy(second, second_v, local_sem.at[2])
    own_copy.start()

    barrier = pltpu.get_barrier_semaphore()
    for shift in (1, WAYS - 1):
        pl.semaphore_signal(
            barrier, inc=1, device_id={"dp": lax.rem(y + shift, WAYS)}, device_id_type=MESH
        )

    def greet(offset, carry):
        pl.semaphore_signal(
            barrier, inc=1, device_id={"fsdp": lax.rem(me + offset, OWNERS)}, device_id_type=MESH
        )
        return carry

    lax.fori_loop(1, OWNERS, greet, 0)
    stat_copy.start()
    second_copy.start()
    pl.semaphore_wait(barrier, OWNERS + 1)

    def group(way, distance):
        return lax.rem(y + (distance if way == 0 else WAYS - distance), WAYS)

    def column(place):
        half = lax.div(place + 1, 2)
        return lax.rem(z + 4 + half * (1 - 2 * lax.rem(place, 2)) + RINGS, RINGS)

    def ring(way, index, source, target):
        return pltpu.make_async_remote_copy(
            src_ref=source,
            dst_ref=target,
            send_sem=ring_send.at[way, index],
            recv_sem=ring_recv.at[way, index],
            device_id={"dp": group(way, 1)},
            device_id_type=MESH,
        )

    def mine(way, distance, place):
        return own[group(way, distance), :, column(place)].astype(F32)

    def hop1(way, j):
        place = j + 4 * way
        return ring(way, j, grad.at[group(way, 4), :, column(place)], r1.at[way, j])

    def hop2_leaf(way, j):
        place = j + 4 * (1 - way)
        return ring(way, 4 + j, grad.at[group(way, 3), :, column(place)], leaf.at[way, j])

    def hop2(way, j):
        return ring(way, 8 + j, s2.at[way, j], r2.at[way, j])

    def hop3(way, j):
        return ring(way, 12 + j, r2.at[way, j], r3.at[way, j + 4 * way])

    def hop3_leaf(way, j):
        return ring(way, 16 + j, s3.at[way, j], r3.at[way, j + 4 * (1 - way)])

    def hop4(way, place):
        return ring(way, 20 + place, r3.at[way, place], r4.at[way, place])

    def each(count, fn):
        def one(j, carry):
            fn(j)
            return carry

        lax.fori_loop(0, count, one, 0)

    def start1(j):
        hop1(0, j).start()
        hop1(1, j).start()

    def start2_leaf(j):
        hop2_leaf(0, j).start()
        hop2_leaf(1, j).start()

    each(4, start1)
    each(4, start2_leaf)
    own_copy.wait()

    def start2(j):
        for way in (0, 1):
            hop1(way, j).wait_recv()
            s2[way, j] = r1[way, j].astype(F32) + mine(way, 3, j + 4 * way)
            hop2(way, j).start()

    each(4, start2)

    def long3(way, j):
        hop2(way, j).wait_recv()
        r2[way, j] = r2[way, j] + mine(way, 2, j + 4 * way)
        hop3(way, j).start()

    def short3(way, j):
        hop2_leaf(way, j).wait_recv()
        s3[way, j] = leaf[way, j].astype(F32) + mine(way, 2, j + 4 * (1 - way))
        hop3_leaf(way, j).start()

    def start3_low(j):
        short3(1, j)
        long3(0, j)

    def start3_high(j):
        short3(0, j)
        long3(1, j)

    each(4, start3_low)
    each(4, start3_high)

    def step4(way, place, arrival):
        arrival.wait_recv()
        r3[way, place] = r3[way, place] + mine(way, 1, place)
        hop4(way, place).start()

    def start4_low(j):
        step4(0, j, hop3(0, j))
        step4(1, j, hop3_leaf(1, j))

    def start4_high(j):
        step4(0, j + 4, hop3_leaf(0, j))
        step4(1, j + 4, hop3(1, j))

    each(4, start4_low)
    each(4, start4_high)
    second_copy.wait()

    def rows_to(target, source):
        return pltpu.make_async_remote_copy(
            src_ref=source,
            dst_ref=gathered.at[me],
            send_sem=row_send,
            recv_sem=row_recv,
            device_id={"fsdp": target},
            device_id_type=MESH,
        )

    sublane = lax.broadcasted_iota(jnp.int32, (COLS, 16, LANES), 1)

    def finish(place):
        hop4(0, place).wait_recv()
        hop4(1, place).wait_recv()
        col = column(place)
        total = r4[0, place] + r4[1, place] + own[y, :, col].astype(F32)
        mean = total * (1.0 / WAYS)
        new = moment_decay * second_v[:, col] + (1.0 - moment_decay) * mean * mean
        moment_v[:, col] = new
        adam = mean / (jnp.sqrt(new) + adam_eps)
        square = adam * adam
        parts = [mean[:, :, c * LANES:(c + 1) * LANES] for c in range(4)]
        squares = [square[:, :, c * LANES:(c + 1) * LANES] for c in range(4)]
        lanes = jnp.sum((squares[0] + squares[1]) + (squares[2] + squares[3]), axis=1, keepdims=True)
        high = lanes.astype(BF16).astype(F32)
        rest = lanes - high
        mid = rest.astype(BF16).astype(F32)
        low = rest - mid
        extra = jnp.where(
            sublane == 0, high, jnp.where(sublane == 1, mid, jnp.where(sublane == 2, low, 0.0))
        )
        outgoing[place] = jnp.concatenate(parts + [extra], axis=1).astype(BF16)
        for index in range(2 * COLS):
            target = 2 * ((index // 2) * RINGS + col) + index % 2
            source = outgoing.at[place, index // 2]

            @pl.when(target != me)
            def _():
                rows_to(target, source).start()

            @pl.when(target == me)
            def _():
                pltpu.make_async_copy(source, gathered.at[me], row_recv).start()

    each(8, finish)
    moment_copy = pltpu.make_async_copy(moment_v, moment, local_sem.at[3])
    moment_copy.start()
    stat_copy.wait()
    pltpu.make_async_copy(gathered, gathered, row_recv).wait()

    def tiles(fn, height=TILE, count=SIZE // TILE, start=0):
        def one(t, carry):
            return fn(pl.multiple_of(t * height, height), carry)

        return lax.fori_loop(0, count, one, start)

    def assemble(t, total):
        piece = gathered[pl.ds(t * 8, 8)].astype(F32)
        for c in range(4):
            part = piece[:, c * ROWS:(c + 1) * ROWS].reshape(TILE, LANES)
            block[pl.ds(pl.multiple_of(t * TILE, TILE), TILE), c * LANES:(c + 1) * LANES] = part.astype(BF16)
        return total + jnp.sum(piece[:, 32:40], axis=0)

    adam_sq = lax.fori_loop(0, SIZE // TILE, assemble, jnp.zeros((ROWS, LANES), F32))
    adam_sq = jnp.sum(adam_sq, keepdims=True)

    @pl.when(core == 0)
    def _():
        p_f[...] = lax.dot_general(
            block[...], block[...], (((1,), (1,)), ((), ())), preferred_element_type=F32
        )

    @pl.when(core == 1)
    def _():
        p_f[...] = lax.dot_general(
            block[...], block[...], (((0,), (0,)), ((), ())), preferred_element_type=F32
        )

    def statistic(t, total):
        here = pl.ds(t, TILE)
        value = stat_decay * stat_v[here] + (1.0 - stat_decay) * p_f[here]
        stat_v[here] = value
        square = value * value
        return total + jnp.sum(square.reshape(TILE // ROWS, ROWS, SIZE), axis=0)

    norm = tiles(statistic, start=jnp.zeros((ROWS, SIZE), F32))
    frobenius = jnp.sqrt(jnp.sum(norm, keepdims=True))
    scaling = 5.0 / (2.0 * frobenius)
    first = jnp.sqrt(jnp.sqrt(scaling))

    def halves(value):
        high = value.astype(BF16)
        return high, (value - high.astype(F32)).astype(BF16)

    def put_left(ref, t, value):
        high, low = halves(value)
        here = pl.ds(t, TILE)
        ref[here, 0:SIZE] = high
        ref[here, SIZE:2 * SIZE] = low
        ref[here, 2 * SIZE:3 * SIZE] = high

    def put_right(ref, t, value):
        high, low = halves(value)
        ref[pl.ds(t, TILE)] = high
        ref[pl.ds(SIZE + t, TILE)] = high
        ref[pl.ds(2 * SIZE + t, TILE)] = low

    def product(left, right):
        q_f[...] = jnp.dot(left[...], right[...], preferred_element_type=F32)

    def scaled(t, carry):
        here = pl.ds(t, TILE)
        value = scaling * stat_v[here]
        a_f[here] = value
        put_left(a_l, t, value)
        put_right(t_r, t, value)
        return carry

    def next_moment(m_ref, left, keep):
        product(left, t_r)

        def squared(t, carry):
            here = pl.ds(t, TILE)
            square = q_f[here]
            value = m_ref[here]
            r_f[here] = 1.5625 * value - 0.625 * square
            put_left(b_l, t, 0.0625 * square - 0.625 * value)
            put_right(u_r, t, square)
            return carry

        tiles(squared)
        product(left, u_r)

        def cubed(t, carry):
            here = pl.ds(t, TILE)
            value = r_f[here] + 0.0625 * q_f[here]
            r_f[here] = value
            put_right(t_r, t, value)
            return carry

        tiles(cubed)
        product(b_l, t_r)

        def last(t, carry):
            here = pl.ds(t, TILE)
            value = 1.5625 * r_f[here] + q_f[here]
            put_right(t_r, t, value)
            if keep:
                m_f[here] = value
                put_left(m_l, t, value)
            return carry

        tiles(last)

    def identity(t, scale):
        row = lax.broadcasted_iota(jnp.int32, (TILE, SIZE), 0) + t
        lane = lax.broadcasted_iota(jnp.int32, (TILE, SIZE), 1)
        return jnp.where(row == lane, scale, 0.0)

    def first_iterate(t):
        return identity(t, 1.25) - 0.25 * a_f[pl.ds(t, TILE)]

    tiles(scaled)
    next_moment(a_f, a_l, True)
    product(a_l, t_r)

    def second_iterate(t, carry):
        here = pl.ds(t, TILE)
        value = 1.25 * first_iterate(t) - 0.25 * (1.25 * m_f[here] - 0.25 * q_f[here])
        x_f[here] = value
        put_left(x_l, t, value)
        return carry

    tiles(second_iterate)
    next_moment(m_f, m_l, False)
    product(x_l, t_r)
    count = steps[0]

    def choose(t, carry):
        here = pl.ds(t, TILE)
        third = 1.25 * x_f[here] - 0.25 * q_f[here]
        value = jnp.where(count == 1, first_iterate(t), jnp.where(count == 2, x_f[here], third))
        roots[core, here] = (first * value).astype(BF16)
        return carry

    tiles(choose)

    swap = pltpu.make_async_remote_copy(
        src_ref=roots.at[core],
        dst_ref=roots.at[core],
        send_sem=root_send,
        recv_sem=root_recv,
        device_id={"fsdp": me + 1 - 2 * core},
        device_id_type=MESH,
    )
    arrival = pltpu.make_async_remote_copy(
        src_ref=roots.at[1 - core],
        dst_ref=roots.at[1 - core],
        send_sem=root_send,
        recv_sem=root_recv,
        device_id={"fsdp": me + 1 - 2 * core},
        device_id_type=MESH,
    )
    swap.start()
    arrival.wait_recv()
    middle[...] = jnp.dot(roots[0], block[...], preferred_element_type=F32).astype(BF16)
    q_f[...] = jnp.dot(middle[...], roots[1], preferred_element_type=F32)

    def rounded(t, total):
        here = pl.ds(t, TILE)
        value = q_f[here].astype(BF16).astype(F32)
        direction[here] = value
        square = value * value
        return total + jnp.sum(square.reshape(TILE // ROWS, ROWS, SIZE), axis=0)

    dir_sq = tiles(rounded, start=jnp.zeros((ROWS, SIZE), F32))
    dir_sq = jnp.sum(dir_sq, keepdims=True)
    ratio = jnp.sqrt(adam_sq) / (jnp.sqrt(dir_sq) + ratio_eps)

    def scale(t, carry):
        here = pl.ds(pl.multiple_of(core * (SIZE // 2) + t * TILE, TILE), TILE)
        value = direction[here] * ratio
        parts = [
            value[:, c * LANES:(c + 1) * LANES].reshape(TILE // ROWS, ROWS, LANES) for c in range(4)
        ]
        back[pl.ds(t * 8, 8)] = jnp.concatenate(parts, axis=1).astype(BF16)
        return carry

    lax.fori_loop(0, SIZE // 2 // TILE, scale, 0)

    def back_to(target, source):
        return pltpu.make_async_remote_copy(
            src_ref=source,
            dst_ref=upd.at[chip],
            send_sem=back_send,
            recv_sem=back_recv,
            device_id={"fsdp": target},
            device_id_type=MESH,
        )

    def give(offset):
        slot = lax.rem(lax.rem(me, HALF) + offset, HALF)
        target = core * HALF + slot
        source = back.at[slot]

        @pl.when(target != me)
        def _():
            back_to(target, source).start()

        @pl.when(target == me)
        def _():
            pltpu.make_async_copy(source, upd.at[chip], back_recv).start()

    each(HALF, give)

    def drain(j):
        for way in (0, 1):
            hop1(way, j).wait_send()
            hop2_leaf(way, j).wait_send()
            hop2(way, j).wait_send()
            hop3(way, j).wait_send()
            hop3_leaf(way, j).wait_send()
            hop4(way, j).wait_send()
            hop4(way, j + 4).wait_send()

    each(4, drain)
    swap.wait_send()
    moment_copy.wait()
    sent = gathered.at[pl.ds(0, OWNERS - 1)]
    pltpu.make_async_copy(sent, sent, row_send).wait()
    returns = lax.div(me, HALF) == core

    @pl.when(returns)
    def _():
        sent_back = back.at[pl.ds(0, HALF - 1)]
        pltpu.make_async_copy(sent_back, sent_back, back_send).wait()

    @pl.when(jnp.logical_not(returns))
    def _():
        pltpu.make_async_copy(back, back, back_send).wait()

    pltpu.make_async_copy(back, upd, back_recv).wait()


def on_device(gradients, statistics, newton_steps, second_moment):
    chunk = (COLS, ROWS, SIZE)
    dma = pltpu.SemaphoreType.DMA
    square_f = pltpu.VMEM((SIZE, SIZE), F32)
    square_b = pltpu.VMEM((SIZE, SIZE), BF16)
    left = pltpu.VMEM((SIZE, 3 * SIZE), BF16)
    right = pltpu.VMEM((3 * SIZE, SIZE), BF16)
    anywhere = pl.BlockSpec(memory_space=pl.ANY)
    upd, moment = pl.pallas_call(
        kernel,
        out_shape=(
            jax.ShapeDtypeStruct((HALF, 32, LANES), BF16),
            jax.ShapeDtypeStruct((COLS, RINGS, ROWS, SIZE), F32),
        ),
        in_specs=[anywhere, anywhere, pl.BlockSpec(memory_space=pltpu.SMEM), anywhere],
        out_specs=(anywhere, anywhere),
        scratch_shapes=[
            pltpu.VMEM((WAYS, COLS, RINGS, ROWS, SIZE), BF16),
            square_f,
            pltpu.VMEM((COLS, RINGS, ROWS, SIZE), F32),
            pltpu.VMEM((COLS, RINGS, ROWS, SIZE), F32),
            pltpu.VMEM((2, 4) + chunk, BF16),
            pltpu.VMEM((2, 4) + chunk, BF16),
            pltpu.VMEM((2, 4) + chunk, F32),
            pltpu.VMEM((2, 4) + chunk, F32),
            pltpu.VMEM((2, 4) + chunk, F32),
            pltpu.VMEM((2, 8) + chunk, F32),
            pltpu.VMEM((2, 8) + chunk, F32),
            pltpu.VMEM((RINGS, COLS, MSG, LANES), BF16),
            pltpu.VMEM((OWNERS, MSG, LANES), BF16),
            square_b,
            square_b,
            square_f,
            pltpu.VMEM((HALF, 32, LANES), BF16),
            pltpu.VMEM((2, SIZE, SIZE), BF16),
        ]
        + [square_f] * 6
        + [left] * 4
        + [right] * 2
        + [
            dma((4,)), dma((2, 28)), dma((2, 28)), dma, dma, dma, dma, dma, dma,
        ],
        compiler_params=pltpu.CompilerParams(
            collective_id=0, has_side_effects=True, vmem_limit_bytes=56 * 2**20
        ),
    )(
        gradients.reshape(WAYS, COLS, RINGS, ROWS, SIZE),
        statistics.reshape(SIZE, SIZE),
        newton_steps,
        second_moment.reshape(COLS, RINGS, ROWS, SIZE),
    )
    update = upd.reshape(HALF, 4, ROWS, LANES).transpose(0, 2, 1, 3).reshape(HALF, ROWS, SIZE)
    return update, moment.reshape(HALF, ROWS, SIZE)


def solution(mesh):
    return jax.shard_map(
        on_device,
        mesh=mesh,
        in_specs=(
            P("dp", None, "fsdp", None),
            P(("dp", "fsdp"), None, None),
            P(("dp", "fsdp")),
            P("dp", "fsdp", None),
        ),
        out_specs=(P("dp", "fsdp", None), P("dp", "fsdp", None)),
        check_vma=False,
    )
```

time: 290 us -> 94.5 us (0.33)
  blocking collectives: 149 us -> 0 us
  Pallas kernels: 0 us -> 89.5 us
  waiting for transfers between devices: 82.1 us -> 0 us
  starting transfers between devices: 21.6 us -> 0 us
  between operations: 15 us -> 1.28 us
  matrix products: 9.55 us -> 0 us
  other arithmetic: 8.15 us -> 0 us
    psum x1 -> x0, blocking collectives: 124 us -> none  [on_device(): adam_sq, dir_sq = lax.psum((adam_part, dir_part), 'fsdp')]
    pallas_call x0 -> x1, Pallas kernels: none -> 89.5 us  [on_device(): pl.pallas_call(kernel, out_shape=(jax.ShapeDtypeStruct((HALF, 32, LANES),...]
    reduce_scatter x1 -> x0, waiting for transfers between devices: 63.3 us -> none  [on_device(): lax.psum_scatter(gradients[0].astype(jnp.float32), 'dp', scatter_dimensio...]
    all_to_all x1 -> x0, blocking collectives: 25.2 us -> none  [on_device(): lax.all_to_all(pieces, 'fsdp', split_axis=0, concat_axis=0, tiled=True)]
    all_to_all x1 -> x0, waiting for transfers between devices: 17.3 us -> none  [on_device(): lax.all_to_all(doubled, 'fsdp', split_axis=0, concat_axis=1, tiled=True)[0]]
    all_to_all x1 -> x0, starting transfers between devices: 11 us -> none  [on_device(): lax.all_to_all(doubled, 'fsdp', split_axis=0, concat_axis=1, tiled=True)[0]]
    ppermute x1 -> x0, starting transfers between devices: 10.6 us -> none  [from_partner(): return lax.ppermute(value, axis, pairs)]
    dot_general x6 -> x0, matrix products: 9.55 us -> none  [the longest x1 1.92 us: one_step(): square = jnp.dot(factor, factor, precision=HIGH)]
  transfers between devices with their start and end apart: 3 -> 0, of which waited for: 3 -> 0; matrix products, arithmetic and copies ran while one was open for 0% -> 0% of each run, Pallas kernels for 0% -> 0%
where the time goes in v1:
time: 94.5 us; the launch traced here: 94.3 us
  Pallas kernels  89.5 us (95%)
  local copies, waits for them, and re-layouts  3.54 us (4%)
  between operations  1.28 us (1%)
    pallas_call x1, Pallas kernels, on_device(): pl.pallas_call(kernel, out_shape=(jax.ShapeDtypeStruct((HALF, 32, LANES),...  89.5 us
    unnamed x2, local copies, waits for them, and re-layouts  3.54 us

profile of v1, /device:TPU:1, one launch (start us, length us, event | category | flops | bytes accessed | tf_op | source)
XLA Modules:
  0.0 94.3 jit_solution(7126086795748232538)
XLA Ops:
  1.3 89.5 %shard_map.59 = (bf16[32,32,128]{2,1,0:T(8,128)(2,1)}, f32[4,8,8,512]{3,2,1,0:T(8,128)}) custom-call(bf16[8,4,8,8,512]{4,3,2,1,0:T(8,128)(2,1)} %bitcast.9, f32[512,512]{1,0:T(8,128)} %bitcast.10, s32[1]{0:T(128)S(6)} %copy.8.steps, f32[4,8,8,512]{3,2,1,0:T(8,128)} %bitcast.12), custom_call_target="tpu_custom_call" | custom-call | tf_op jit(solution)/shard_map/pallas_call | solution.py:464
  90.8 1.7 %copy.9 = bf16[32,8,512]{2,1,0:T(8,128)(2,1)} copy(bf16[32,8,512]{2,1,0:T(8,128)(2,1)} %bitcast.13) | data formatting | bytes 524288
  92.4 1.9 %copy.10 = f32[32,8,512]{2,1,0:T(8,128)} copy(f32[32,8,512]{2,1,0:T(8,128)} %bitcast.11) | data formatting | bytes 1048576

commit v2 on v1

v2 whole, which is shorter than its diff:
```python
import jax
import jax.numpy as jnp
from jax import lax
from jax.experimental import pallas as pl
from jax.experimental.pallas import tpu as pltpu
from jax.sharding import PartitionSpec as P

stat_decay = 0.9
moment_decay = 0.95
adam_eps = 1e-08
ratio_eps = 1e-06
MESH = pl.DeviceIdType.MESH
F32 = jnp.float32
BF16 = jnp.bfloat16
LANES = 128
ROWS = 8
TILE = 64
SIZE = 512
WAYS = 8
COLS = 4
RINGS = 8
OWNERS = 64
HALF = OWNERS // 2
PART = 256


def kernel(
    grad, stats, steps, second, upd, moment,
    own, stat_v, second_v, moment_v,
    r1, leaf, r2, s2, s3, r3, r4,
    outgoing, gathered, sums_out, sums_in, block, middle, back, roots,
    a_f, p_f, q_f, m_f, n_f,
    a_l, b_l, m_l, n_l, u_l, ra, rb, rc,
    local_sem, ring_send, ring_recv, row_send, row_recv, pair_send, pair_recv,
    sum_send, sum_recv, root_send, root_recv, back_send, back_recv,
):
    y = lax.axis_index("dp")
    me = lax.axis_index("fsdp")
    core = lax.rem(me, 2)
    chip = lax.div(me, 2)
    x = lax.div(chip, RINGS)
    z = lax.rem(chip, RINGS)
    partner = me + 1 - 2 * core

    def each(count, fn, first=0):
        def one(j, carry):
            fn(j)
            return carry

        lax.fori_loop(first, count, one, 0)

    barrier = pltpu.get_barrier_semaphore()
    for shift in (1, WAYS - 1):
        pl.semaphore_signal(
            barrier, inc=1, device_id={"dp": lax.rem(y + shift, WAYS)}, device_id_type=MESH
        )

    def greet(t):
        offset = lax.rem(t, COLS) * 2 * RINGS + lax.div(t, COLS)
        pl.semaphore_signal(
            barrier, inc=1, device_id={"fsdp": lax.rem(me + offset, OWNERS)}, device_id_type=MESH
        )

    each(OWNERS, greet, 1)
    own_copy = pltpu.make_async_copy(grad, own, local_sem.at[0])
    stat_copy = pltpu.make_async_copy(stats, stat_v, local_sem.at[1])
    second_copy = pltpu.make_async_copy(second, second_v, local_sem.at[2])
    own_copy.start()
    second_copy.start()
    stat_copy.start()
    pl.semaphore_wait(barrier, OWNERS + 1)

    def group(way, distance):
        return lax.rem(y + (distance if way == 0 else WAYS - distance), WAYS)

    def shift_of(place):
        half = lax.div(place + 1, 2)
        return 4 + half * (1 - 2 * lax.rem(place, 2))

    def column(place):
        return lax.rem(z + shift_of(place), RINGS)

    def ring(way, index, source, target):
        return pltpu.make_async_remote_copy(
            src_ref=source,
            dst_ref=target,
            send_sem=ring_send.at[way],
            recv_sem=ring_recv.at[way, index],
            device_id={"dp": group(way, 1)},
            device_id_type=MESH,
        )

    def mine(way, distance, place):
        return own[group(way, distance), :, column(place)].astype(F32)

    def hop1(way, j):
        place = j + 4 * way
        return ring(way, j, grad.at[group(way, 4), :, column(place)], r1.at[way, j])

    def hop2_leaf(way, j):
        place = j + 4 * (1 - way)
        return ring(way, 4 + j, grad.at[group(way, 3), :, column(place)], leaf.at[way, j])

    def hop2(way, j):
        return ring(way, 8 + j, s2.at[way, j], r2.at[way, j])

    def hop3(way, j):
        return ring(way, 12 + j, r2.at[way, j], r3.at[way, j + 4 * way])

    def hop3_leaf(way, j):
        return ring(way, 16 + j, s3.at[way, j], r3.at[way, j + 4 * (1 - way)])

    def hop4(way, place):
        return ring(way, 20 + place, r3.at[way, place], r4.at[way, place])

    def start1(j):
        hop1(0, j).start()
        hop1(1, j).start()

    def start2_leaf(j):
        hop2_leaf(0, j).start()
        hop2_leaf(1, j).start()

    each(4, start1)
    each(4, start2_leaf)
    own_copy.wait()

    def start2(j):
        for way in (0, 1):
            hop1(way, j).wait_recv()
            s2[way, j] = r1[way, j].astype(F32) + mine(way, 3, j + 4 * way)
            hop2(way, j).start()

    each(4, start2)

    def long3(way, j):
        hop2(way, j).wait_recv()
        r2[way, j] = r2[way, j] + mine(way, 2, j + 4 * way)
        hop3(way, j).start()

    def short3(way, j):
        hop2_leaf(way, j).wait_recv()
        s3[way, j] = leaf[way, j].astype(F32) + mine(way, 2, j + 4 * (1 - way))
        hop3_leaf(way, j).start()

    def start3_low(j):
        short3(1, j)
        long3(0, j)

    def start3_high(j):
        short3(0, j)
        long3(1, j)

    each(4, start3_low)
    each(4, start3_high)

    def step4(way, place, arrival):
        arrival.wait_recv()
        r3[way, place] = r3[way, place] + mine(way, 1, place)
        hop4(way, place).start()

    def start4_low(j):
        step4(0, j, hop3(0, j))
        step4(1, j, hop3_leaf(1, j))

    def start4_high(j):
        step4(0, j + 4, hop3_leaf(0, j))
        step4(1, j + 4, hop3(1, j))

    each(4, start4_low)
    each(4, start4_high)
    second_copy.wait()

    def finish(place):
        hop4(0, place).wait_recv()
        hop4(1, place).wait_recv()
        col = column(place)
        total = r4[0, place] + r4[1, place] + own[y, :, col].astype(F32)
        mean = total * (1.0 / WAYS)
        new = moment_decay * second_v[:, col] + (1.0 - moment_decay) * mean * mean
        moment_v[:, col] = new
        adam = mean / (jnp.sqrt(new) + adam_eps)
        square = adam * adam
        parts = [mean[:, :, c * LANES:(c + 1) * LANES] for c in range(4)]
        squares = [square[:, :, c * LANES:(c + 1) * LANES] for c in range(4)]
        outgoing[place] = jnp.concatenate(parts, axis=1).astype(BF16)
        for index in range(COLS):
            target = 2 * (index * RINGS + col) + core
            source = outgoing.at[place, index]

            @pl.when(target != me)
            def _():
                pltpu.make_async_remote_copy(
                    src_ref=source,
                    dst_ref=gathered.at[core, place, x],
                    send_sem=row_send,
                    recv_sem=row_recv.at[place],
                    device_id={"fsdp": target},
                    device_id_type=MESH,
                ).start()

            @pl.when(target == me)
            def _():
                pltpu.make_async_copy(source, gathered.at[core, place, x], row_recv.at[place]).start()

        sums_out[place] = jnp.sum(
            (squares[0] + squares[1]) + (squares[2] + squares[3]), axis=1, keepdims=True
        )
        for index in range(2 * COLS):
            target = 2 * ((index // 2) * RINGS + col) + index % 2
            source = sums_out.at[place, index // 2]

            @pl.when(target != me)
            def _():
                pltpu.make_async_remote_copy(
                    src_ref=source,
                    dst_ref=sums_in.at[me],
                    send_sem=sum_send,
                    recv_sem=sum_recv,
                    device_id={"fsdp": target},
                    device_id_type=MESH,
                ).start()

            @pl.when(target == me)
            def _():
                pltpu.make_async_copy(source, sums_in.at[me], sum_recv).start()

    each(8, finish)
    moment_copy = pltpu.make_async_copy(moment_v, moment, local_sem.at[3])
    moment_copy.start()

    def to_partner(source, target, send, recv):
        return pltpu.make_async_remote_copy(
            src_ref=source,
            dst_ref=target,
            send_sem=send,
            recv_sem=recv,
            device_id={"fsdp": partner},
            device_id_type=MESH,
        )

    def forward(place):
        here = gathered.at[core, place]
        pltpu.make_async_copy(here, here, row_recv.at[place]).wait()
        to_partner(here, here, pair_send, pair_recv).start()

    each(8, forward)
    stat_copy.wait()
    there = gathered.at[1 - core]
    pltpu.make_async_copy(there, there, pair_recv).wait()

    def assemble(place):
        source_z = lax.rem(z + RINGS - shift_of(place) + RINGS, RINGS)
        for index in range(COLS):
            pair = [gathered[c, place, index].astype(F32) for c in (0, 1)]
            start = pl.multiple_of((index * RINGS + source_z) * 16, 16)
            for c in range(4):
                both = [p[c * ROWS:(c + 1) * ROWS] for p in pair]
                block[pl.ds(start, 16), c * LANES:(c + 1) * LANES] = jnp.concatenate(both, axis=0).astype(BF16)

    each(8, assemble)

    @pl.when(core == 0)
    def _():
        p_f[...] = lax.dot_general(
            block[...], block[...], (((1,), (1,)), ((), ())), preferred_element_type=F32
        )

    @pl.when(core == 1)
    def _():
        p_f[...] = lax.dot_general(
            block[...], block[...], (((0,), (0,)), ((), ())), preferred_element_type=F32
        )

    def square_sum(value):
        return jnp.sum((value * value).reshape(value.shape[0] // ROWS, ROWS, SIZE), axis=0)

    norm = jnp.zeros((ROWS, SIZE), F32)
    for t in range(0, SIZE, TILE):
        here = slice(t, t + TILE)
        value = stat_decay * stat_v[here] + (1.0 - stat_decay) * p_f[here]
        stat_v[here] = value
        norm = norm + square_sum(value)
    frobenius = jnp.sqrt(jnp.sum(norm, keepdims=True))
    scaling = 5.0 / (2.0 * frobenius)
    first = jnp.sqrt(jnp.sqrt(scaling))

    def halves(value):
        high = value.astype(BF16)
        return high, (value - high.astype(F32)).astype(BF16)

    def put_left(ref, t, parts):
        high, low = parts
        here = slice(t, t + TILE)
        ref[here, 0:SIZE] = high
        ref[here, SIZE:2 * SIZE] = low
        ref[here, 2 * SIZE:3 * SIZE] = high

    def put_right(ref, t, parts):
        high, low = parts
        ref[t:t + TILE] = high
        ref[SIZE + t:SIZE + t + TILE] = high
        ref[2 * SIZE + t:2 * SIZE + t + TILE] = low

    def product(left, right, use):
        for h in range(0, SIZE, PART):
            q_f[h:h + PART] = jnp.dot(left[h:h + PART], right[...], preferred_element_type=F32)
            for t in range(h, h + PART, TILE):
                use(t, slice(t, t + TILE), q_f[t:t + TILE])

    def identity(t, scale):
        row = lax.broadcasted_iota(jnp.int32, (TILE, SIZE), 0) + t
        lane = lax.broadcasted_iota(jnp.int32, (TILE, SIZE), 1)
        return jnp.where(row == lane, scale, 0.0)

    for t in range(0, SIZE, TILE):
        here = slice(t, t + TILE)
        value = scaling * stat_v[here]
        a_f[here] = value
        parts = halves(value)
        put_left(a_l, t, parts)
        put_right(ra, t, parts)

    def squared(t, here, q):
        p_f[here] = q
        put_left(b_l, t, halves(0.0625 * q - 0.625 * a_f[here]))
        put_right(rb, t, halves(q))

    def cubed(t, here, q):
        value = 1.5625 * a_f[here] - 0.625 * p_f[here] + 0.0625 * q
        n_f[here] = value
        put_right(rc, t, halves(value))

    def moved(t, here, q):
        value = 1.5625 * n_f[here] + q
        m_f[here] = value
        parts = halves(value)
        put_left(m_l, t, parts)
        put_right(ra, t, parts)

    def squared_again(t, here, q):
        m = m_f[here]
        value = 1.25 * m - 0.25 * q
        n_f[here] = value
        put_left(n_l, t, halves(value))
        put_right(rb, t, halves(0.0625 * q - 0.625 * m))

    def fourth(t, here, q):
        value = 1.5625 * n_f[here] + q
        p_f[here] = value
        put_left(u_l, t, halves(value))

    count = steps[0]

    def last_factor(t, here, q):
        second_w = identity(t, 1.25) - 0.25 * m_f[here]
        third = 1.25 * second_w - 0.25 * (1.5625 * p_f[here] + q)
        value = jnp.where(count == 2, second_w, third)
        n_f[here] = value
        put_right(rc, t, halves(value))

    def swap_half(h):
        here = roots.at[core, pl.ds(h * PART, PART)]
        return to_partner(here, here, root_send.at[h], root_recv.at[h])

    def swapped_half(h):
        here = roots.at[1 - core, pl.ds(h * PART, PART)]
        return to_partner(here, here, root_send.at[h], root_recv.at[h])

    def choose(t, here, q):
        one = identity(t, 1.25) - 0.25 * a_f[here]
        more = 1.25 * n_f[here] - 0.25 * q
        value = jnp.where(count == 1, one, more)
        roots[core, here] = (first * value).astype(BF16)
        if (t + TILE) % PART == 0:
            swap_half(t // PART).start()

    product(a_l, ra, squared)
    product(a_l, rb, cubed)
    product(b_l, rc, moved)
    product(m_l, ra, squared_again)
    product(n_l, rb, fourth)
    product(u_l, rb, last_factor)
    product(a_l, rc, choose)

    adam_sums = sums_in.at[...]
    pltpu.make_async_copy(adam_sums, adam_sums, sum_recv).wait()
    adam_sq = jnp.sum(jnp.sum(sums_in[...], axis=0), keepdims=True)
    for h in (0, 1):
        @pl.when(core == 1)
        def _():
            swapped_half(h).wait_recv()

        here = slice(h * PART, (h + 1) * PART)
        middle[here] = jnp.dot(roots[0, here], block[...], preferred_element_type=F32).astype(BF16)

    @pl.when(core == 0)
    def _():
        swapped_half(0).wait_recv()
        swapped_half(1).wait_recv()

    dir_sq = jnp.zeros((ROWS, SIZE), F32)
    for h in range(0, SIZE, PART):
        q_f[h:h + PART] = jnp.dot(middle[h:h + PART], roots[1], preferred_element_type=F32)
        for t in range(h, h + PART, TILE):
            here = slice(t, t + TILE)
            value = q_f[here].astype(BF16).astype(F32)
            q_f[here] = value
            dir_sq = dir_sq + square_sum(value)
    dir_sq = jnp.sum(dir_sq, keepdims=True)
    ratio = jnp.sqrt(adam_sq) / (jnp.sqrt(dir_sq) + ratio_eps)

    def scale(t):
        here = pl.ds(pl.multiple_of(core * PART + t * TILE, TILE), TILE)
        value = q_f[here] * ratio
        parts = [
            value[:, c * LANES:(c + 1) * LANES].reshape(TILE // ROWS, ROWS, LANES) for c in range(4)
        ]
        back[pl.ds(t * 8, 8)] = jnp.concatenate(parts, axis=1).astype(BF16)
        for index in range(8):
            slot = t * 8 + index
            target = core * HALF + slot
            source = back.at[slot]

            @pl.when(target != me)
            def _():
                pltpu.make_async_remote_copy(
                    src_ref=source,
                    dst_ref=upd.at[chip],
                    send_sem=back_send,
                    recv_sem=back_recv,
                    device_id={"fsdp": target},
                    device_id_type=MESH,
                ).start()

            @pl.when(target == me)
            def _():
                pltpu.make_async_copy(source, upd.at[chip], back_recv).start()

    each(PART // TILE, scale)

    for way in (0, 1):
        sent = own.at[pl.ds(0, 6)]
        pltpu.make_async_copy(sent, sent, ring_send.at[way]).wait()
    swap_half(0).wait_send()
    swap_half(1).wait_send()
    here = gathered.at[core]
    pltpu.make_async_copy(here, here, pair_send).wait()
    sent = back.at[pl.ds(0, HALF - 1)]
    pltpu.make_async_copy(sent, sent, row_send).wait()
    sent_sums = sums_in.at[pl.ds(0, OWNERS - 1)]
    pltpu.make_async_copy(sent_sums, sent_sums, sum_send).wait()
    moment_copy.wait()
    returns = lax.div(me, HALF) == core

    @pl.when(returns)
    def _():
        sent_back = back.at[pl.ds(0, HALF - 1)]
        pltpu.make_async_copy(sent_back, sent_back, back_send).wait()

    @pl.when(jnp.logical_not(returns))
    def _():
        pltpu.make_async_copy(back, back, back_send).wait()

    pltpu.make_async_copy(back, upd, back_recv).wait()


def write_out(upd, moment_in, update, moment, upd_v, update_v, moment_v, sems):
    rows_in = pltpu.make_async_copy(upd, upd_v, sems.at[0])
    moment_here = pltpu.make_async_copy(moment_in, moment_v, sems.at[1])
    rows_in.start()
    moment_here.start()
    moment_here.wait()
    moment_out = pltpu.make_async_copy(moment_v, moment, sems.at[2])
    moment_out.start()
    rows_in.wait()
    wide = upd_v[...].astype(F32)
    for c in range(4):
        update_v[:, :, c * LANES:(c + 1) * LANES] = wide[:, c * ROWS:(c + 1) * ROWS].astype(BF16)
    rows_out = pltpu.make_async_copy(update_v, update, sems.at[3])
    rows_out.start()
    moment_out.wait()
    rows_out.wait()


def on_device(gradients, statistics, newton_steps, second_moment):
    chunk = (COLS, ROWS, SIZE)
    dma = pltpu.SemaphoreType.DMA
    square_f = pltpu.VMEM((SIZE, SIZE), F32)
    square_b = pltpu.VMEM((SIZE, SIZE), BF16)
    left = pltpu.VMEM((SIZE, 3 * SIZE), BF16)
    right = pltpu.VMEM((3 * SIZE, SIZE), BF16)
    anywhere = pl.BlockSpec(memory_space=pl.ANY)
    group_f = pltpu.VMEM((COLS, RINGS, ROWS, SIZE), F32)
    upd, moment = pl.pallas_call(
        kernel,
        out_shape=(
            jax.ShapeDtypeStruct((HALF, 32, LANES), BF16),
            jax.ShapeDtypeStruct((COLS, RINGS, ROWS, SIZE), F32),
        ),
        in_specs=[anywhere, anywhere, pl.BlockSpec(memory_space=pltpu.SMEM), anywhere],
        out_specs=(anywhere, anywhere),
        scratch_shapes=[
            pltpu.VMEM((WAYS, COLS, RINGS, ROWS, SIZE), BF16),
            square_f,
            group_f,
            group_f,
            pltpu.VMEM((2, 4) + chunk, BF16),
            pltpu.VMEM((2, 4) + chunk, BF16),
            pltpu.VMEM((2, 4) + chunk, F32),
            pltpu.VMEM((2, 4) + chunk, F32),
            pltpu.VMEM((2, 4) + chunk, F32),
            pltpu.VMEM((2, 8) + chunk, F32),
            pltpu.VMEM((2, 8) + chunk, F32),
            pltpu.VMEM((RINGS, COLS, 32, LANES), BF16),
            pltpu.VMEM((2, RINGS, COLS, 32, LANES), BF16),
            pltpu.VMEM((RINGS, COLS, 1, LANES), F32),
            pltpu.VMEM((OWNERS, 1, LANES), F32),
            square_b,
            square_b,
            pltpu.VMEM((HALF, 32, LANES), BF16),
            pltpu.VMEM((2, SIZE, SIZE), BF16),
        ]
        + [square_f] * 5
        + [left] * 5
        + [right] * 3
        + [
            dma((4,)), dma((2,)), dma((2, 28)), dma, dma((8,)), dma, dma,
            dma, dma, dma((2,)), dma((2,)), dma, dma,
        ],
        compiler_params=pltpu.CompilerParams(
            collective_id=0, has_side_effects=True, vmem_limit_bytes=56 * 2**20
        ),
    )(
        gradients.reshape(WAYS, COLS, RINGS, ROWS, SIZE),
        statistics.reshape(SIZE, SIZE),
        newton_steps,
        second_moment.reshape(COLS, RINGS, ROWS, SIZE),
    )
    return pl.pallas_call(
        write_out,
        out_shape=(
            jax.ShapeDtypeStruct((HALF, ROWS, SIZE), BF16),
            jax.ShapeDtypeStruct((HALF, ROWS, SIZE), F32),
        ),
        in_specs=[anywhere, anywhere],
        out_specs=(anywhere, anywhere),
        scratch_shapes=[
            pltpu.VMEM((HALF, 32, LANES), BF16),
            pltpu.VMEM((HALF, ROWS, SIZE), BF16),
            pltpu.VMEM((HALF, ROWS, SIZE), F32),
            dma((4,)),
        ],
    )(upd, moment.reshape(HALF, ROWS, SIZE))


def solution(mesh):
    return jax.shard_map(
        on_device,
        mesh=mesh,
        in_specs=(
            P("dp", None, "fsdp", None),
            P(("dp", "fsdp"), None, None),
            P(("dp", "fsdp")),
            P("dp", "fsdp", None),
        ),
        out_specs=(P("dp", "fsdp", None), P("dp", "fsdp", None)),
        check_vma=False,
    )
```

time: 94.5 us -> 78 us (0.83)
  Pallas kernels: 89.5 us -> 76.1 us
  local copies, waits for them, and re-layouts: 3.54 us -> 0 us
    pallas_call x1, Pallas kernels: 89.5 us -> 74 us  [on_device(): pl.pallas_call(kernel, out_shape=(jax.ShapeDtypeStruct((HALF, 32, LANES),...]
    unnamed x2 -> x0, local copies, waits for them, and re-layouts: 3.54 us -> none
    pallas_call x0 -> x1, Pallas kernels: none -> 2.03 us  [on_device(): pl.pallas_call(write_out, out_shape=(jax.ShapeDtypeStruct((HALF, ROWS, SI...]
where the time goes in v2:
time: 78 us; the launch traced here: 77.3 us
  Pallas kernels  76.1 us (98%)
  between operations  1.28 us (2%)
    pallas_call x1, Pallas kernels, on_device(): pl.pallas_call(kernel, out_shape=(jax.ShapeDtypeStruct((HALF, 32, LANES),...  74 us
    pallas_call x1, Pallas kernels, on_device(): pl.pallas_call(write_out, out_shape=(jax.ShapeDtypeStruct((HALF, ROWS, SI...  2.03 us

profile of v2, /device:TPU:1, one launch (start us, length us, event | category | flops | bytes accessed | tf_op | source)
XLA Modules:
  0.0 77.3 jit_solution(16742315595764849192)
XLA Ops:
  1.3 74.0 %shard_map.59 = (bf16[32,32,128]{2,1,0:T(8,128)(2,1)}, f32[4,8,8,512]{3,2,1,0:T(8,128)}) custom-call(bf16[8,4,8,8,512]{4,3,2,1,0:T(8,128)(2,1)} %bitcast.4, f32[512,512]{1,0:T(8,128)} %bitcast.5, s32[1]{0:T(128)S(6)} %copy.6.steps, f32[4,8,8,512]{3,2,1,0:T(8,128)} %bitcast.7), custom_call_target="tpu_custom_call" | custom-call | tf_op jit(solution)/shard_map/pallas_call | solution.py:495
  75.3 2.0 %shard_map.60 = (bf16[32,8,512]{2,1,0:T(8,128)(2,1)}, f32[32,8,512]{2,1,0:T(8,128)}) custom-call(bf16[32,32,128]{2,1,0:T(8,128)(2,1)} %get-tuple-element.4.upd, f32[32,8,512]{2,1,0:T(8,128)} %bitcast.6), custom_call_target="tpu_custom_call" | custom-call | tf_op jit(solution)/shard_map/pallas_call | solution.py:540

commit v3 on v2

--- a/solution.py
+++ b/solution.py
@@ -27,11 +27,11 @@
 def kernel(
     grad, stats, steps, second, upd, moment,
     own, stat_v, second_v, moment_v,
-    r1, leaf, r2, s2, s3, r3, r4,
+    r1, leaf, codes_out, codes_in, units_out, units_in, steps_v,
     outgoing, gathered, sums_out, sums_in, block, middle, back, roots,
     a_f, p_f, q_f, m_f, n_f,
     a_l, b_l, m_l, n_l, u_l, ra, rb, rc,
-    local_sem, ring_send, ring_recv, row_send, row_recv, pair_send, pair_recv,
+    local_sem, raw_send, raw_recv, code_send, code_recv, unit_send, unit_recv, row_send, row_recv, pair_send, pair_recv,
     sum_send, sum_recv, root_send, root_recv, back_send, back_recv,
 ):
     y = lax.axis_index("dp")
@@ -65,9 +65,11 @@
     own_copy = pltpu.make_async_copy(grad, own, local_sem.at[0])
     stat_copy = pltpu.make_async_copy(stats, stat_v, local_sem.at[1])
     second_copy = pltpu.make_async_copy(second, second_v, local_sem.at[2])
+    steps_copy = pltpu.make_async_copy(steps, steps_v, local_sem.at[4])
     own_copy.start()
     second_copy.start()
     stat_copy.start()
+    steps_copy.start()
     pl.semaphore_wait(barrier, OWNERS + 1)
 
     def group(way, distance):
@@ -80,38 +82,65 @@
     def column(place):
         return lax.rem(z + shift_of(place), RINGS)
 
-    def ring(way, index, source, target):
+    def ring(way, source, target, send, recv):
         return pltpu.make_async_remote_copy(
             src_ref=source,
             dst_ref=target,
-            send_sem=ring_send.at[way],
-            recv_sem=ring_recv.at[way, index],
+            send_sem=send,
+            recv_sem=recv,
             device_id={"dp": group(way, 1)},
             device_id_type=MESH,
         )
 
+    def raw(way, index, distance, place, target):
+        source = grad.at[group(way, distance), :, column(place)]
+        return ring(way, source, target, raw_send.at[way], raw_recv.at[way, index])
+
+    def hop1(way, j):
+        return raw(way, j, 4, j + 4 * way, r1.at[way, j])
+
+    def hop2_leaf(way, j):
+        return raw(way, 4 + j, 3, j + 4 * (1 - way), leaf.at[way, j])
+
+    def codes(way, index):
+        return ring(
+            way, codes_out.at[way, index], codes_in.at[way, index], code_send.at[way], code_recv.at[way, index]
+        )
+
+    def units(way, index):
+        return ring(
+            way, units_out.at[way, index], units_in.at[way, index], unit_send.at[way], unit_recv.at[way, index]
+        )
+
+    def near_power(value):
+        wide = value * (2.0**23 + 1.0)
+        return wide - (wide - value)
+
+    def columns_of(value):
+        return [value[:, :, c * LANES:(c + 1) * LANES] for c in range(4)]
+
+    def send_sum(way, index, value):
+        parts = columns_of(value)
+        size = [jnp.abs(part) for part in parts]
+        largest = jnp.maximum(jnp.maximum(size[0], size[1]), jnp.maximum(size[2], size[3]))
+        largest = jnp.maximum(jnp.max(largest, axis=1, keepdims=True), 1e-25)
+        power = near_power(largest)
+        units_out[way, index] = power * 2.0**-14
+        units(way, index).start()
+        inverse = near_power(2.0**14 / power)
+        near = [(part * inverse + 1.5 * 2.0**23) - 1.5 * 2.0**23 for part in parts]
+        codes_out[way, index] = jnp.concatenate(near, axis=2).astype(jnp.int32).astype(jnp.int16)
+        codes(way, index).start()
+
+    def received(way, index):
+        units(way, index).wait_recv()
+        codes(way, index).wait_recv()
+        unit = units_in[way, index]
+        parts = columns_of(codes_in[way, index].astype(jnp.int32).astype(F32))
+        return jnp.concatenate([part * unit for part in parts], axis=2)
+
     def mine(way, distance, place):
         return own[group(way, distance), :, column(place)].astype(F32)
-
-    def hop1(way, j):
-        place = j + 4 * way
-        return ring(way, j, grad.at[group(way, 4), :, column(place)], r1.at[way, j])
-
-    def hop2_leaf(way, j):
-        place = j + 4 * (1 - way)
-        return ring(way, 4 + j, grad.at[group(way, 3), :, column(place)], leaf.at[way, j])
-
-    def hop2(way, j):
-        return ring(way, 8 + j, s2.at[way, j], r2.at[way, j])
-
-    def hop3(way, j):
-        return ring(way, 12 + j, r2.at[way, j], r3.at[way, j + 4 * way])
-
-    def hop3_leaf(way, j):
-        return ring(way, 16 + j, s3.at[way, j], r3.at[way, j + 4 * (1 - way)])
-
-    def hop4(way, place):
-        return ring(way, 20 + place, r3.at[way, place], r4.at[way, place])
 
     def start1(j):
         hop1(0, j).start()
@@ -128,20 +157,18 @@
     def start2(j):
         for way in (0, 1):
             hop1(way, j).wait_recv()
-            s2[way, j] = r1[way, j].astype(F32) + mine(way, 3, j + 4 * way)
-            hop2(way, j).start()
+            send_sum(way, j, r1[way, j].astype(F32) + mine(way, 3, j + 4 * way))
 
     each(4, start2)
 
     def long3(way, j):
-        hop2(way, j).wait_recv()
-        r2[way, j] = r2[way, j] + mine(way, 2, j + 4 * way)
-        hop3(way, j).start()
+        place = j + 4 * way
+        send_sum(way, 4 + place, received(way, j) + mine(way, 2, place))
 
     def short3(way, j):
+        place = j + 4 * (1 - way)
         hop2_leaf(way, j).wait_recv()
-        s3[way, j] = leaf[way, j].astype(F32) + mine(way, 2, j + 4 * (1 - way))
-        hop3_leaf(way, j).start()
+        send_sum(way, 4 + place, leaf[way, j].astype(F32) + mine(way, 2, place))
 
     def start3_low(j):
         short3(1, j)
@@ -154,36 +181,23 @@
     each(4, start3_low)
     each(4, start3_high)
 
-    def step4(way, place, arrival):
-        arrival.wait_recv()
-        r3[way, place] = r3[way, place] + mine(way, 1, place)
-        hop4(way, place).start()
-
-    def start4_low(j):
-        step4(0, j, hop3(0, j))
-        step4(1, j, hop3_leaf(1, j))
-
-    def start4_high(j):
-        step4(0, j + 4, hop3_leaf(0, j))
-        step4(1, j + 4, hop3(1, j))
-
-    each(4, start4_low)
-    each(4, start4_high)
+    def start4(place):
+        for way in (0, 1):
+            send_sum(way, 12 + place, received(way, 4 + place) + mine(way, 1, place))
+
+    each(8, start4)
     second_copy.wait()
 
     def finish(place):
-        hop4(0, place).wait_recv()
-        hop4(1, place).wait_recv()
         col = column(place)
-        total = r4[0, place] + r4[1, place] + own[y, :, col].astype(F32)
+        total = received(0, 12 + place) + received(1, 12 + place) + own[y, :, col].astype(F32)
         mean = total * (1.0 / WAYS)
         new = moment_decay * second_v[:, col] + (1.0 - moment_decay) * mean * mean
         moment_v[:, col] = new
         adam = mean / (jnp.sqrt(new) + adam_eps)
         square = adam * adam
-        parts = [mean[:, :, c * LANES:(c + 1) * LANES] for c in range(4)]
-        squares = [square[:, :, c * LANES:(c + 1) * LANES] for c in range(4)]
-        outgoing[place] = jnp.concatenate(parts, axis=1).astype(BF16)
+        squares = columns_of(square)
+        outgoing[place] = jnp.concatenate(columns_of(mean), axis=1).astype(BF16)
         for index in range(COLS):
             target = 2 * (index * RINGS + col) + core
             source = outgoing.at[place, index]
@@ -273,7 +287,7 @@
         )
 
     def square_sum(value):
-        return jnp.sum((value * value).reshape(value.shape[0] // ROWS, ROWS, SIZE), axis=0)
+        return jnp.sum((value * value).reshape(value.shape[0] // ROWS, ROWS, value.shape[1]), axis=0)
 
     norm = jnp.zeros((ROWS, SIZE), F32)
     for t in range(0, SIZE, TILE):
@@ -289,91 +303,95 @@
         high = value.astype(BF16)
         return high, (value - high.astype(F32)).astype(BF16)
 
-    def put_left(ref, t, parts):
+    def put_left(ref, t, cols, parts):
         high, low = parts
         here = slice(t, t + TILE)
-        ref[here, 0:SIZE] = high
-        ref[here, SIZE:2 * SIZE] = low
-        ref[here, 2 * SIZE:3 * SIZE] = high
-
-    def put_right(ref, t, parts):
+        for shift, part in ((0, high), (SIZE, low), (2 * SIZE, high)):
+            ref[here, cols.start + shift:cols.stop + shift] = part
+
+    def put_right(ref, t, cols, parts):
         high, low = parts
-        ref[t:t + TILE] = high
-        ref[SIZE + t:SIZE + t + TILE] = high
-        ref[2 * SIZE + t:2 * SIZE + t + TILE] = low
+        for shift, part in ((0, high), (SIZE, high), (2 * SIZE, low)):
+            ref[t + shift:t + shift + TILE, cols] = part
 
     def product(left, right, use):
         for h in range(0, SIZE, PART):
-            q_f[h:h + PART] = jnp.dot(left[h:h + PART], right[...], preferred_element_type=F32)
-            for t in range(h, h + PART, TILE):
-                use(t, slice(t, t + TILE), q_f[t:t + TILE])
-
-    def identity(t, scale):
-        row = lax.broadcasted_iota(jnp.int32, (TILE, SIZE), 0) + t
-        lane = lax.broadcasted_iota(jnp.int32, (TILE, SIZE), 1)
+            cols = slice(h, h + PART)
+            q_f[:, cols] = jnp.dot(left[...], right[:, cols], preferred_element_type=F32)
+            for t in range(0, SIZE, TILE):
+                here = (slice(t, t + TILE), cols)
+                use(t, cols, here, q_f[here])
+
+    def identity(t, cols, scale):
+        shape = (TILE, cols.stop - cols.start)
+        row = lax.broadcasted_iota(jnp.int32, shape, 0) + t
+        lane = lax.broadcasted_iota(jnp.int32, shape, 1) + cols.start
         return jnp.where(row == lane, scale, 0.0)
 
+    everything = slice(0, SIZE)
     for t in range(0, SIZE, TILE):
         here = slice(t, t + TILE)
         value = scaling * stat_v[here]
         a_f[here] = value
         parts = halves(value)
-        put_left(a_l, t, parts)
-        put_right(ra, t, parts)
-
-    def squared(t, here, q):
+        put_left(a_l, t, everything, parts)
+        put_right(ra, t, everything, parts)
+
+    def squared(t, cols, here, q):
         p_f[here] = q
-        put_left(b_l, t, halves(0.0625 * q - 0.625 * a_f[here]))
-        put_right(rb, t, halves(q))
-
-    def cubed(t, here, q):
+        put_left(b_l, t, cols, halves(0.0625 * q - 0.625 * a_f[here]))
+        put_right(rb, t, cols, halves(q))
+
+    def cubed(t, cols, here, q):
         value = 1.5625 * a_f[here] - 0.625 * p_f[here] + 0.0625 * q
         n_f[here] = value
-        put_right(rc, t, halves(value))
-
-    def moved(t, here, q):
+        put_right(rc, t, cols, halves(value))
+
+    def moved(t, cols, here, q):
         value = 1.5625 * n_f[here] + q
         m_f[here] = value
         parts = halves(value)
-        put_left(m_l, t, parts)
-        put_right(ra, t, parts)
-
-    def squared_again(t, here, q):
+        put_left(m_l, t, cols, parts)
+        put_right(ra, t, cols, parts)
+
+    def squared_again(t, cols, here, q):
         m = m_f[here]
         value = 1.25 * m - 0.25 * q
         n_f[here] = value
-        put_left(n_l, t, halves(value))
-        put_right(rb, t, halves(0.0625 * q - 0.625 * m))
-
-    def fourth(t, here, q):
+        put_left(n_l, t, cols, halves(value))
+        put_right(rb, t, cols, halves(0.0625 * q - 0.625 * m))
+
+    def fourth(t, cols, here, q):
         value = 1.5625 * n_f[here] + q
         p_f[here] = value
-        put_left(u_l, t, halves(value))
-
-    count = steps[0]
-
-    def last_factor(t, here, q):
-        second_w = identity(t, 1.25) - 0.25 * m_f[here]
+        put_left(u_l, t, cols, halves(value))
+
+    steps_copy.wait()
+    count = steps_v[0]
+
+    def last_factor(t, cols, here, q):
+        second_w = identity(t, cols, 1.25) - 0.25 * m_f[here]
         third = 1.25 * second_w - 0.25 * (1.5625 * p_f[here] + q)
         value = jnp.where(count == 2, second_w, third)
         n_f[here] = value
-        put_right(rc, t, halves(value))
+        put_right(rc, t, cols, halves(value))
 
     def swap_half(h):
-        here = roots.at[core, pl.ds(h * PART, PART)]
+        here = roots.at[core, h]
         return to_partner(here, here, root_send.at[h], root_recv.at[h])
 
     def swapped_half(h):
-        here = roots.at[1 - core, pl.ds(h * PART, PART)]
+        here = roots.at[1 - core, h]
         return to_partner(here, here, root_send.at[h], root_recv.at[h])
 
-    def choose(t, here, q):
-        one = identity(t, 1.25) - 0.25 * a_f[here]
+    def choose(t, cols, here, q):
+        one = identity(t, cols, 1.25) - 0.25 * a_f[here]
         more = 1.25 * n_f[here] - 0.25 * q
         value = jnp.where(count == 1, one, more)
-        roots[core, here] = (first * value).astype(BF16)
-        if (t + TILE) % PART == 0:
-            swap_half(t // PART).start()
+        h = cols.start // PART
+        roots[core, h, t:t + TILE] = (first * value).astype(BF16)
+        if t + TILE == SIZE:
+            swap_half(h).start()
 
     product(a_l, ra, squared)
     product(a_l, rb, cubed)
@@ -386,26 +404,27 @@
     adam_sums = sums_in.at[...]
     pltpu.make_async_copy(adam_sums, adam_sums, sum_recv).wait()
     adam_sq = jnp.sum(jnp.sum(sums_in[...], axis=0), keepdims=True)
-    for h in (0, 1):
-        @pl.when(core == 1)
-        def _():
-            swapped_half(h).wait_recv()
-
-        here = slice(h * PART, (h + 1) * PART)
-        middle[here] = jnp.dot(roots[0, here], block[...], preferred_element_type=F32).astype(BF16)
-
-    @pl.when(core == 0)
+    @pl.when(core == 1)
     def _():
         swapped_half(0).wait_recv()
         swapped_half(1).wait_recv()
 
-    dir_sq = jnp.zeros((ROWS, SIZE), F32)
-    for h in range(0, SIZE, PART):
-        q_f[h:h + PART] = jnp.dot(middle[h:h + PART], roots[1], preferred_element_type=F32)
-        for t in range(h, h + PART, TILE):
+    total = jnp.dot(roots[0, 0], block[0:PART], preferred_element_type=F32)
+    total = total + jnp.dot(roots[0, 1], block[PART:SIZE], preferred_element_type=F32)
+    middle[...] = total.astype(BF16)
+
+    dir_sq = jnp.zeros((ROWS, PART), F32)
+    for h in (0, 1):
+        @pl.when(core == 0)
+        def _():
+            swapped_half(h).wait_recv()
+
+        cols = slice(h * PART, (h + 1) * PART)
+        q_f[:, cols] = jnp.dot(middle[...], roots[1, h], preferred_element_type=F32)
+        for t in range(0, SIZE, TILE):
             here = slice(t, t + TILE)
-            value = q_f[here].astype(BF16).astype(F32)
-            q_f[here] = value
+            value = q_f[here, cols].astype(BF16).astype(F32)
+            q_f[here, cols] = value
             dir_sq = dir_sq + square_sum(value)
     dir_sq = jnp.sum(dir_sq, keepdims=True)
     ratio = jnp.sqrt(adam_sq) / (jnp.sqrt(dir_sq) + ratio_eps)
@@ -440,8 +459,10 @@
     each(PART // TILE, scale)
 
     for way in (0, 1):
-        sent = own.at[pl.ds(0, 6)]
-        pltpu.make_async_copy(sent, sent, ring_send.at[way]).wait()
+        sent_raw = own.at[0]
+        pltpu.make_async_copy(sent_raw, sent_raw, raw_send.at[way]).wait()
+        pltpu.make_async_copy(codes_out.at[way], codes_out.at[way], code_send.at[way]).wait()
+        pltpu.make_async_copy(units_out.at[way], units_out.at[way], unit_send.at[way]).wait()
     swap_half(0).wait_send()
     swap_half(1).wait_send()
     here = gathered.at[core]
@@ -498,7 +519,7 @@
             jax.ShapeDtypeStruct((HALF, 32, LANES), BF16),
             jax.ShapeDtypeStruct((COLS, RINGS, ROWS, SIZE), F32),
         ),
-        in_specs=[anywhere, anywhere, pl.BlockSpec(memory_space=pltpu.SMEM), anywhere],
+        in_specs=[anywhere] * 4,
         out_specs=(anywhere, anywhere),
         scratch_shapes=[
             pltpu.VMEM((WAYS, COLS, RINGS, ROWS, SIZE), BF16),
@@ -507,11 +528,11 @@
             group_f,
             pltpu.VMEM((2, 4) + chunk, BF16),
             pltpu.VMEM((2, 4) + chunk, BF16),
-            pltpu.VMEM((2, 4) + chunk, F32),
-            pltpu.VMEM((2, 4) + chunk, F32),
-            pltpu.VMEM((2, 4) + chunk, F32),
-            pltpu.VMEM((2, 8) + chunk, F32),
-            pltpu.VMEM((2, 8) + chunk, F32),
+            pltpu.VMEM((2, 20) + chunk, jnp.int16),
+            pltpu.VMEM((2, 20) + chunk, jnp.int16),
+            pltpu.VMEM((2, 20, COLS, 1, LANES), F32),
+            pltpu.VMEM((2, 20, COLS, 1, LANES), F32),
+            pltpu.SMEM((1,), jnp.int32),
             pltpu.VMEM((RINGS, COLS, 32, LANES), BF16),
             pltpu.VMEM((2, RINGS, COLS, 32, LANES), BF16),
             pltpu.VMEM((RINGS, COLS, 1, LANES), F32),
@@ -519,13 +540,14 @@
             square_b,
             square_b,
             pltpu.VMEM((HALF, 32, LANES), BF16),
-            pltpu.VMEM((2, SIZE, SIZE), BF16),
+            pltpu.VMEM((2, 2, SIZE, PART), BF16),
         ]
         + [square_f] * 5
         + [left] * 5
         + [right] * 3
         + [
-            dma((4,)), dma((2,)), dma((2, 28)), dma, dma((8,)), dma, dma,
+            dma((5,)), dma((2,)), dma((2, 8)), dma((2,)), dma((2, 20)), dma((2,)), dma((2, 20)),
+            dma, dma((8,)), dma, dma,
             dma, dma, dma((2,)), dma((2,)), dma, dma,
         ],
         compiler_params=pltpu.CompilerParams(

time: 78 us -> 67.8 us (0.87)
  Pallas kernels: 76.1 us -> 65.6 us
    pallas_call x1, Pallas kernels: 74 us -> 63.6 us  [on_device(): pl.pallas_call(kernel, out_shape=(jax.ShapeDtypeStruct((HALF, 32, LANES),...]
where the time goes in v3:
time: 67.8 us; the launch traced here: 66.9 us
  Pallas kernels  65.6 us (97%)
  between operations  1.28 us (2%)
    pallas_call x1, Pallas kernels, on_device(): pl.pallas_call(kernel, out_shape=(jax.ShapeDtypeStruct((HALF, 32, LANES),...  63.6 us
    pallas_call x1, Pallas kernels, on_device(): pl.pallas_call(write_out, out_shape=(jax.ShapeDtypeStruct((HALF, ROWS, SI...  2.03 us

profile of v3, /device:TPU:1, one launch (start us, length us, event | category | flops | bytes accessed | tf_op | source)
XLA Modules:
  0.0 66.9 jit_solution(11815340567788709447)
XLA Ops:
  1.3 63.6 %shard_map.59 = (bf16[32,32,128]{2,1,0:T(8,128)(2,1)}, f32[4,8,8,512]{3,2,1,0:T(8,128)}) custom-call(bf16[8,4,8,8,512]{4,3,2,1,0:T(8,128)(2,1)} %bitcast.4, f32[512,512]{1,0:T(8,128)} %bitcast.5, s32[1]{0:T(128)S(6)} %copy.6.steps, f32[4,8,8,512]{3,2,1,0:T(8,128)} %bitcast.7), custom_call_target="tpu_custom_call" | custom-call | tf_op jit(solution)/shard_map/pallas_call | solution.py:516
  64.9 2.0 %shard_map.60 = (bf16[32,8,512]{2,1,0:T(8,128)(2,1)}, f32[32,8,512]{2,1,0:T(8,128)}) custom-call(bf16[32,32,128]{2,1,0:T(8,128)(2,1)} %get-tuple-element.4.upd, f32[32,8,512]{2,1,0:T(8,128)} %bitcast.6), custom_call_target="tpu_custom_call" | custom-call | tf_op jit(solution)/shard_map/pallas_call | solution.py:562

commit v4 on v3

v4 whole, which is shorter than its diff:
```python
import jax
import jax.numpy as jnp
from jax import lax
from jax.experimental import pallas as pl
from jax.experimental.pallas import tpu as pltpu
from jax.sharding import PartitionSpec as P

stat_decay = 0.9
moment_decay = 0.95
adam_eps = 1e-08
ratio_eps = 1e-06
MESH = pl.DeviceIdType.MESH
F32 = jnp.float32
BF16 = jnp.bfloat16
LANES = 128
ROWS = 8
TILE = 64
SIZE = 512
WAYS = 8
COLS = 4
RINGS = 8
OWNERS = 64
HALF = OWNERS // 2
PART = 256
FAR = 7


def kernel(
    grad, stats, steps, second, upd, moment,
    own, stat_v, second_v, moment_v,
    r1, leaf, codes_out, codes_in, units_out, units_in, steps_v,
    outgoing, gathered, sums_out, sums_in, adam_pair, block, middle, back, roots,
    a_f, p_f, q_f, m_f, n_f,
    a_b, b_b, p_b, n_b, m_b,
    local_sem, raw_send, raw_recv, code_send, unit_send, sum_over_recv, row_send, row_recv, cross_send, cross_recv,
    pair_send, pair_recv, sum_send, sum_recv, sum_pair_send, sum_pair_recv, root_send, root_recv,
    back_send, back_recv,
):
    y = lax.axis_index("dp")
    me = lax.axis_index("fsdp")
    core = lax.rem(me, 2)
    chip = lax.div(me, 2)
    x = lax.div(chip, RINGS)
    z = lax.rem(chip, RINGS)
    partner = me + 1 - 2 * core

    def each(count, fn, first=0):
        def one(j, carry):
            fn(j)
            return carry

        lax.fori_loop(first, count, one, 0)

    barrier = pltpu.get_barrier_semaphore()
    for shift in (1, WAYS - 1):
        pl.semaphore_signal(
            barrier, inc=1, device_id={"dp": lax.rem(y + shift, WAYS)}, device_id_type=MESH
        )

    def hello(target):
        pl.semaphore_signal(barrier, inc=1, device_id={"fsdp": target}, device_id_type=MESH)

    for turn in range(1, COLS):
        hello(lax.rem(me + 2 * RINGS * turn, OWNERS))

    def greet(t):
        low = lax.rem(me + t, 2 * RINGS)
        for high in range(COLS):
            hello(2 * RINGS * high + low)

    each(2 * RINGS, greet, 1)
    own_copy = pltpu.make_async_copy(grad, own, local_sem.at[0])
    stat_copy = pltpu.make_async_copy(stats, stat_v, local_sem.at[1])
    second_copy = pltpu.make_async_copy(second, second_v, local_sem.at[2])
    steps_copy = pltpu.make_async_copy(steps, steps_v, local_sem.at[4])
    own_copy.start()
    second_copy.start()
    stat_copy.start()
    steps_copy.start()
    pl.semaphore_wait(barrier, OWNERS + 1)

    def group(way, distance):
        return lax.rem(y + (distance if way == 0 else WAYS - distance), WAYS)

    def shift_of(place):
        half = lax.div(place + 1, 2)
        return 4 + half * (1 - 2 * lax.rem(place, 2))

    def column(place):
        return lax.rem(z + shift_of(place), RINGS)

    def ring(way, source, target, send, recv):
        return pltpu.make_async_remote_copy(
            src_ref=source,
            dst_ref=target,
            send_sem=send,
            recv_sem=recv,
            device_id={"dp": group(way, 1)},
            device_id_type=MESH,
        )

    def raw(way, index, distance, place, target):
        source = grad.at[group(way, distance), :, column(place)]
        return ring(way, source, target, raw_send.at[way], raw_recv.at[way, index])

    def long_place(way, batch, i):
        return 4 * batch + 2 * way + i

    def short_place(way, batch, i):
        return 4 * batch + 2 * (1 - way) + i

    def hop1(way, batch, i):
        index = 2 * batch + i
        return raw(way, index, 4, long_place(way, batch, i), r1.at[way, index])

    def hop2_leaf(way, batch, i):
        index = 2 * batch + i
        return raw(way, 4 + index, 3, short_place(way, batch, i), leaf.at[way, index])

    def codes(way, index):
        return ring(
            way, codes_out.at[way, index], codes_in.at[way, index], code_send.at[way], sum_over_recv.at[way, index]
        )

    def units(way, index):
        return ring(
            way, units_out.at[way, index], units_in.at[way, index], unit_send.at[way], sum_over_recv.at[way, index]
        )

    def near_power(value):
        wide = value * (2.0**23 + 1.0)
        return wide - (wide - value)

    def columns_of(value):
        return [value[:, :, c * LANES:(c + 1) * LANES] for c in range(4)]

    def send_sum(way, index, value):
        parts = columns_of(value)
        size = [jnp.abs(part) for part in parts]
        largest = jnp.maximum(jnp.maximum(size[0], size[1]), jnp.maximum(size[2], size[3]))
        largest = jnp.maximum(jnp.max(largest, axis=1, keepdims=True), 1e-25)
        power = near_power(largest)
        units_out[way, index] = power * 2.0**-14
        units(way, index).start()
        inverse = near_power(2.0**14 / power)
        near = [(part * inverse + 1.5 * 2.0**23) - 1.5 * 2.0**23 for part in parts]
        codes_out[way, index] = jnp.concatenate(near, axis=2).astype(jnp.int32).astype(jnp.int16)
        codes(way, index).start()

    def received(way, index):
        both = units_in.at[0, pl.ds(0, 17)]
        pltpu.make_async_copy(both, both, sum_over_recv.at[way, index]).wait()
        unit = units_in[way, index]
        parts = columns_of(codes_in[way, index].astype(jnp.int32).astype(F32))
        return jnp.concatenate([part * unit for part in parts], axis=2)

    def mine(way, distance, place):
        return own[group(way, distance), :, column(place)].astype(F32)

    def both_ways(batch, fn):
        def one(i):
            for way in (0, 1):
                fn(way, batch, i)

        each(2, one)

    def start1(way, batch, i):
        hop1(way, batch, i).start()

    def start2_leaf(way, batch, i):
        hop2_leaf(way, batch, i).start()

    def start2(way, batch, i):
        index = 2 * batch + i
        hop1(way, batch, i).wait_recv()
        send_sum(way, index, r1[way, index].astype(F32) + mine(way, 3, long_place(way, batch, i)))

    def short3(way, batch, i):
        place = short_place(way, batch, i)
        hop2_leaf(way, batch, i).wait_recv()
        send_sum(way, 4 + place, leaf[way, 2 * batch + i].astype(F32) + mine(way, 2, place))

    def long3(way, batch, i):
        place = long_place(way, batch, i)
        send_sum(way, 4 + place, received(way, 2 * batch + i) + mine(way, 2, place))

    def last4(way, place):
        send_sum(way, 12 + place, received(way, 4 + place) + mine(way, 1, place))

    def short4(way, batch, i):
        last4(way, short_place(way, batch, i))

    def long4(way, batch, i):
        last4(way, long_place(way, batch, i))

    def finish(place):
        col = column(place)
        total = received(0, 12 + place) + received(1, 12 + place) + own[y, :, col].astype(F32)
        mean = total * (1.0 / WAYS)
        new = moment_decay * second_v[:, col] + (1.0 - moment_decay) * mean * mean
        moment_v[:, col] = new
        adam = mean / (jnp.sqrt(new) + adam_eps)
        square = adam * adam
        squares = columns_of(square)
        outgoing[place] = jnp.concatenate(columns_of(mean), axis=1).astype(BF16)
        sums_out[place] = jnp.sum(
            (squares[0] + squares[1]) + (squares[2] + squares[3]), axis=1, keepdims=True
        )
        for index in range(COLS):
            to_owner(
                2 * (index * RINGS + col) + core,
                outgoing.at[place, index],
                gathered.at[core, place, x],
                row_send,
                row_recv.at[place],
            )

    def to_owner(target, source, there, send, recv):
        @pl.when(target != me)
        def _():
            pltpu.make_async_remote_copy(
                src_ref=source,
                dst_ref=there,
                send_sem=send,
                recv_sem=recv,
                device_id={"fsdp": target},
                device_id_type=MESH,
            ).start()

        @pl.when(target == me)
        def _():
            pltpu.make_async_copy(source, there, recv).start()

    def finish_near(place):
        finish(place)
        for index in range(COLS):
            pltpu.make_async_remote_copy(
                src_ref=outgoing.at[place, index],
                dst_ref=gathered.at[core, place, x],
                send_sem=cross_send,
                recv_sem=cross_recv,
                device_id={"fsdp": 2 * (index * RINGS + column(place)) + 1 - core},
                device_id_type=MESH,
            ).start()

    both_ways(0, start1)
    both_ways(0, start2_leaf)
    both_ways(1, start1)
    own_copy.wait()
    both_ways(0, start2)
    both_ways(0, short3)
    both_ways(1, start2_leaf)
    both_ways(0, long3)
    both_ways(0, short4)
    both_ways(1, start2)
    both_ways(0, long4)
    both_ways(1, short3)
    both_ways(1, long3)
    second_copy.wait()
    each(4, finish)
    both_ways(1, short4)
    both_ways(1, long4)
    each(FAR, finish, 4)
    each(RINGS, finish_near, FAR)
    moment_copy = pltpu.make_async_copy(moment_v, moment, local_sem.at[3])
    moment_copy.start()

    def to_partner(source, target, send, recv):
        return pltpu.make_async_remote_copy(
            src_ref=source,
            dst_ref=target,
            send_sem=send,
            recv_sem=recv,
            device_id={"fsdp": partner},
            device_id_type=MESH,
        )

    def forward(place):
        here = gathered.at[core, place]
        pltpu.make_async_copy(here, here, row_recv.at[place]).wait()
        to_partner(here, here, pair_send, pair_recv).start()

    def send_adam(place):
        for index in range(COLS):
            to_owner(
                2 * (index * RINGS + column(place)) + core,
                sums_out.at[place, index],
                sums_in.at[chip],
                sum_send,
                sum_recv,
            )

    each(RINGS, send_adam)
    each(FAR, forward)

    stat_copy.wait()
    for place in range(FAR, RINGS):
        here = gathered.at[core, place]
        pltpu.make_async_copy(here, here, row_recv.at[place]).wait()
    near = gathered.at[1 - core, pl.ds(FAR, RINGS - FAR)]
    pltpu.make_async_copy(near, near, cross_recv).wait()
    there = gathered.at[1 - core, pl.ds(0, FAR)]
    pltpu.make_async_copy(there, there, pair_recv).wait()

    def assemble(place):
        source_z = lax.rem(z + RINGS - shift_of(place) + RINGS, RINGS)
        for index in range(COLS):
            pair = [gathered[c, place, index].astype(F32) for c in (0, 1)]
            start = pl.multiple_of((index * RINGS + source_z) * 16, 16)
            for c in range(4):
                both = [p[c * ROWS:(c + 1) * ROWS] for p in pair]
                block[pl.ds(start, 16), c * LANES:(c + 1) * LANES] = jnp.concatenate(both, axis=0).astype(BF16)

    each(8, assemble)

    @pl.when(core == 0)
    def _():
        p_f[...] = lax.dot_general(
            block[...], block[...], (((1,), (1,)), ((), ())), preferred_element_type=F32
        )

    @pl.when(core == 1)
    def _():
        p_f[...] = lax.dot_general(
            block[...], block[...], (((0,), (0,)), ((), ())), preferred_element_type=F32
        )

    def square_sum(value):
        return jnp.sum((value * value).reshape(value.shape[0] // ROWS, ROWS, value.shape[1]), axis=0)

    def halves(value):
        high = value.astype(BF16)
        return high, (value - high.astype(F32)).astype(BF16)

    def put(ref, here, value):
        high, low = halves(value)
        ref[(0,) + here] = high
        ref[(1,) + here] = low

    def three(left, right, rows, cols):
        def one(a, b):
            return jnp.dot(left[a, rows], right[b, :, cols], preferred_element_type=F32)

        return one(0, 0) + one(1, 0) + one(0, 1)

    low, high = slice(0, PART), slice(PART, SIZE)

    def product(left, right, use):
        def spread(piece, rows, cols):
            for t in range(0, PART, TILE):
                here = slice(rows.start + t, rows.start + t + TILE)
                use(here.start, cols, (here, cols), piece[t:t + TILE])

        corner = three(left, right, low, low)
        side = three(left, right, low, high)
        spread(corner, low, low)
        end = three(left, right, high, high)
        spread(side, low, high)
        spread(side.T, high, low)
        spread(end, high, high)

    def identity(t, cols, scale):
        shape = (TILE, cols.stop - cols.start)
        row = lax.broadcasted_iota(jnp.int32, shape, 0) + t
        lane = lax.broadcasted_iota(jnp.int32, shape, 1) + cols.start
        return jnp.where(row == lane, scale, 0.0)

    everything = slice(0, SIZE)
    norm = jnp.zeros((ROWS, SIZE), F32)
    for t in range(0, SIZE, TILE):
        here = slice(t, t + TILE)
        value = stat_decay * stat_v[here] + (1.0 - stat_decay) * p_f[here]
        a_f[here] = value
        norm = norm + square_sum(value)
        put(a_b, (here, everything), value)
    frobenius = jnp.sqrt(jnp.sum(norm, keepdims=True))
    scaling = 5.0 / (2.0 * frobenius)
    first = jnp.sqrt(jnp.sqrt(scaling))

    def squared(t, cols, here, q):
        value = (q * scaling) * scaling
        p_f[here] = value
        put(b_b, here, 0.0625 * value - (0.625 * scaling) * a_f[here])
        put(p_b, here, value)

    def cubed(t, cols, here, q):
        value = (1.5625 * scaling) * a_f[here] - 0.625 * p_f[here] + (0.0625 * scaling) * q
        n_f[here] = value
        put(n_b, here, value)

    def moved(t, cols, here, q):
        value = 1.5625 * n_f[here] + q
        m_f[here] = value
        put(m_b, here, value)

    def squared_again(t, cols, here, q):
        m = m_f[here]
        value = 1.25 * m - 0.25 * q
        n_f[here] = value
        put(n_b, here, value)
        put(b_b, here, 0.0625 * q - 0.625 * m)

    def fourth(t, cols, here, q):
        value = 1.5625 * n_f[here] + q
        p_f[here] = value
        put(p_b, here, value)

    steps_copy.wait()
    count = steps_v[0]

    def last_factor(t, cols, here, q):
        second_w = identity(t, cols, 1.25) - 0.25 * m_f[here]
        third = 1.25 * second_w - 0.25 * (1.5625 * p_f[here] + q)
        value = jnp.where(count == 2, second_w, third)
        n_f[here] = value
        put(n_b, here, value)

    def swap_half(h):
        here = roots.at[core, h]
        return to_partner(here, here, root_send.at[h], root_recv.at[h])

    def swapped_half(h):
        here = roots.at[1 - core, h]
        return to_partner(here, here, root_send.at[h], root_recv.at[h])

    def choose(t, cols, here, q):
        one = identity(t, cols, 1.25) - (0.25 * scaling) * a_f[here]
        more = 1.25 * n_f[here] - (0.25 * scaling) * q
        value = jnp.where(count == 1, one, more)
        h = cols.start // PART
        roots[core, h, t:t + TILE] = (first * value).astype(BF16)
        if t + TILE == SIZE:
            swap_half(h).start()

    product(a_b, a_b, squared)
    product(a_b, p_b, cubed)
    product(b_b, n_b, moved)
    product(m_b, m_b, squared_again)
    product(n_b, b_b, fourth)
    product(p_b, b_b, last_factor)

    for cols in (low, high):
        last = three(a_b, n_b, slice(0, SIZE), cols)
        for t in range(0, SIZE, TILE):
            choose(t, cols, (slice(t, t + TILE), cols), last[t:t + TILE])

    pltpu.make_async_copy(sums_in, sums_in, sum_recv).wait()
    adam_pair[core] = jnp.sum(sums_in[...], axis=0)
    adam_swap = to_partner(adam_pair.at[core], adam_pair.at[core], sum_pair_send, sum_pair_recv)
    adam_swapped = to_partner(adam_pair.at[1 - core], adam_pair.at[1 - core], sum_pair_send, sum_pair_recv)
    adam_swap.start()
    @pl.when(core == 1)
    def _():
        swapped_half(0).wait_recv()

    total = jnp.dot(roots[0, 0], block[0:PART], preferred_element_type=F32)

    @pl.when(core == 1)
    def _():
        swapped_half(1).wait_recv()

    total = total + jnp.dot(roots[0, 1], block[PART:SIZE], preferred_element_type=F32)
    middle[...] = total.astype(BF16)

    dir_sq = jnp.zeros((ROWS, PART), F32)
    for h in (0, 1):
        @pl.when(core == 0)
        def _():
            swapped_half(h).wait_recv()

        cols = slice(h * PART, (h + 1) * PART)
        q_f[:, cols] = jnp.dot(middle[...], roots[1, h], preferred_element_type=F32)
        for t in range(0, SIZE, TILE):
            here = slice(t, t + TILE)
            value = q_f[here, cols].astype(BF16).astype(F32)
            q_f[here, cols] = value
            dir_sq = dir_sq + square_sum(value)
    dir_sq = jnp.sum(dir_sq, keepdims=True)
    adam_swapped.wait_recv()
    adam_sq = jnp.sum(adam_pair[0] + adam_pair[1], keepdims=True)
    ratio = jnp.sqrt(adam_sq) / (jnp.sqrt(dir_sq) + ratio_eps)

    for t in range(PART // TILE):
        here = pl.ds(pl.multiple_of(core * PART + t * TILE, TILE), TILE)
        value = q_f[here] * ratio
        parts = [
            value[:, c * LANES:(c + 1) * LANES].reshape(TILE // ROWS, ROWS, LANES) for c in range(4)
        ]
        back[t * 8:(t + 1) * 8] = jnp.concatenate(parts, axis=1).astype(BF16)

    def give(row):
        for index in range(COLS):
            slot = 2 * (index // 2 * RINGS + row) + index % 2
            to_owner(core * HALF + slot, back.at[slot], upd.at[chip], back_send, back_recv)

    each(RINGS, give)

    for way in (0, 1):
        sent_raw = own.at[0]
        pltpu.make_async_copy(sent_raw, sent_raw, raw_send.at[way]).wait()
        pltpu.make_async_copy(codes_out.at[way], codes_out.at[way], code_send.at[way]).wait()
        pltpu.make_async_copy(units_out.at[way], units_out.at[way], unit_send.at[way]).wait()
    swap_half(0).wait_send()
    swap_half(1).wait_send()
    here = gathered.at[core, pl.ds(0, FAR)]
    pltpu.make_async_copy(here, here, pair_send).wait()
    here = gathered.at[core, pl.ds(0, RINGS - FAR)]
    pltpu.make_async_copy(here, here, cross_send).wait()
    sent = back.at[pl.ds(0, HALF - 1)]
    pltpu.make_async_copy(sent, sent, row_send).wait()
    sent_sums = sums_in.at[pl.ds(0, HALF - 1)]
    pltpu.make_async_copy(sent_sums, sent_sums, sum_send).wait()
    adam_swap.wait_send()
    moment_copy.wait()
    returns = lax.div(me, HALF) == core

    @pl.when(returns)
    def _():
        sent_back = back.at[pl.ds(0, HALF - 1)]
        pltpu.make_async_copy(sent_back, sent_back, back_send).wait()

    @pl.when(jnp.logical_not(returns))
    def _():
        pltpu.make_async_copy(back, back, back_send).wait()

    pltpu.make_async_copy(back, upd, back_recv).wait()


def write_out(upd, moment_in, update, moment, upd_v, update_v, moment_v, sems):
    def quarter(t):
        return pl.ds(t * 8, 8)

    def come(t):
        here = quarter(t)
        return (
            pltpu.make_async_copy(moment_in.at[here], moment_v.at[here], sems.at[t]),
            pltpu.make_async_copy(upd.at[here], upd_v.at[here], sems.at[4 + t]),
        )

    def go(t):
        here = quarter(t)
        return (
            pltpu.make_async_copy(moment_v.at[here], moment.at[here], sems.at[8 + t]),
            pltpu.make_async_copy(update_v.at[here], update.at[here], sems.at[12 + t]),
        )

    coming = [come(t) for t in range(4)]
    going = [go(t) for t in range(4)]
    for pair in coming:
        for copy in pair:
            copy.start()
    for t in range(4):
        coming[t][0].wait()
        going[t][0].start()
        coming[t][1].wait()
        wide = upd_v[t * 8:(t + 1) * 8].astype(F32)
        for c in range(4):
            update_v[t * 8:(t + 1) * 8, :, c * LANES:(c + 1) * LANES] = wide[:, c * ROWS:(c + 1) * ROWS].astype(BF16)
        going[t][1].start()
    for pair in going:
        for copy in pair:
            copy.wait()


def on_device(gradients, statistics, newton_steps, second_moment):
    chunk = (COLS, ROWS, SIZE)
    dma = pltpu.SemaphoreType.DMA
    square_f = pltpu.VMEM((SIZE, SIZE), F32)
    square_b = pltpu.VMEM((SIZE, SIZE), BF16)
    both = pltpu.VMEM((2, SIZE, SIZE), BF16)
    anywhere = pl.BlockSpec(memory_space=pl.ANY)
    group_f = pltpu.VMEM((COLS, RINGS, ROWS, SIZE), F32)
    upd, moment = pl.pallas_call(
        kernel,
        out_shape=(
            jax.ShapeDtypeStruct((HALF, 32, LANES), BF16),
            jax.ShapeDtypeStruct((COLS, RINGS, ROWS, SIZE), F32),
        ),
        in_specs=[anywhere] * 4,
        out_specs=(anywhere, anywhere),
        scratch_shapes=[
            pltpu.VMEM((WAYS, COLS, RINGS, ROWS, SIZE), BF16),
            square_f,
            group_f,
            group_f,
            pltpu.VMEM((2, 4) + chunk, BF16),
            pltpu.VMEM((2, 4) + chunk, BF16),
            pltpu.VMEM((2, 20) + chunk, jnp.int16),
            pltpu.VMEM((2, 20) + chunk, jnp.int16),
            pltpu.VMEM((2, 20, COLS, 1, LANES), F32),
            pltpu.VMEM((2, 20, COLS, 1, LANES), F32),
            pltpu.SMEM((1,), jnp.int32),
            pltpu.VMEM((RINGS, COLS, 32, LANES), BF16),
            pltpu.VMEM((2, RINGS, COLS, 32, LANES), BF16),
            pltpu.VMEM((RINGS, COLS, 1, LANES), F32),
            pltpu.VMEM((HALF, 1, LANES), F32),
            pltpu.VMEM((2, 1, LANES), F32),
            square_b,
            square_b,
            pltpu.VMEM((HALF, 32, LANES), BF16),
            pltpu.VMEM((2, 2, SIZE, PART), BF16),
        ]
        + [square_f] * 5
        + [both] * 5
        + [
            dma((5,)), dma((2,)), dma((2, 8)), dma((2,)), dma((2,)), dma((2, 20)), dma, dma((8,)), dma, dma,
            dma, dma, dma, dma, dma, dma, dma((2,)), dma((2,)), dma, dma,
        ],
        compiler_params=pltpu.CompilerParams(
            collective_id=0, has_side_effects=True, vmem_limit_bytes=56 * 2**20
        ),
    )(
        gradients.reshape(WAYS, COLS, RINGS, ROWS, SIZE),
        statistics.reshape(SIZE, SIZE),
        newton_steps,
        second_moment.reshape(COLS, RINGS, ROWS, SIZE),
    )
    return pl.pallas_call(
        write_out,
        out_shape=(
            jax.ShapeDtypeStruct((HALF, ROWS, SIZE), BF16),
            jax.ShapeDtypeStruct((HALF, ROWS, SIZE), F32),
        ),
        in_specs=[anywhere, anywhere],
        out_specs=(anywhere, anywhere),
        scratch_shapes=[
            pltpu.VMEM((HALF, 32, LANES), BF16),
            pltpu.VMEM((HALF, ROWS, SIZE), BF16),
            pltpu.VMEM((HALF, ROWS, SIZE), F32),
            dma((16,)),
        ],
    )(upd, moment.reshape(HALF, ROWS, SIZE))


def solution(mesh):
    return jax.shard_map(
        on_device,
        mesh=mesh,
        in_specs=(
            P("dp", None, "fsdp", None),
            P(("dp", "fsdp"), None, None),
            P(("dp", "fsdp")),
            P("dp", "fsdp", None),
        ),
        out_specs=(P("dp", "fsdp", None), P("dp", "fsdp", None)),
        check_vma=False,
    )
```

time: 67.8 us -> 65.7 us (0.969)
  Pallas kernels: 65.6 us -> 64.2 us
    pallas_call x1, Pallas kernels: 63.6 us -> 62.2 us  [on_device(): pl.pallas_call(kernel, out_shape=(jax.ShapeDtypeStruct((HALF, 32, LANES),...]
where the time goes in v4:
time: 65.7 us; the launch traced here: 65.5 us
  Pallas kernels  64.2 us (98%)
  between operations  1.28 us (2%)
    pallas_call x1, Pallas kernels, on_device(): pl.pallas_call(kernel, out_shape=(jax.ShapeDtypeStruct((HALF, 32, LANES),...  62.2 us
    pallas_call x1, Pallas kernels, on_device(): pl.pallas_call(write_out, out_shape=(jax.ShapeDtypeStruct((HALF, ROWS, SI...  2 us

profile of v4, /device:TPU:1, one launch (start us, length us, event | category | flops | bytes accessed | tf_op | source)
XLA Modules:
  0.0 65.5 jit_solution(345914119094427209)
XLA Ops:
  1.3 62.2 %shard_map.59 = (bf16[32,32,128]{2,1,0:T(8,128)(2,1)}, f32[4,8,8,512]{3,2,1,0:T(8,128)}) custom-call(bf16[8,4,8,8,512]{4,3,2,1,0:T(8,128)(2,1)} %bitcast.4, f32[512,512]{1,0:T(8,128)} %bitcast.5, s32[1]{0:T(128)S(6)} %copy.6.steps, f32[4,8,8,512]{3,2,1,0:T(8,128)} %bitcast.7), custom_call_target="tpu_custom_call" | custom-call | tf_op jit(solution)/shard_map/pallas_call | solution.py:573
  63.5 2.0 %shard_map.60 = (bf16[32,8,512]{2,1,0:T(8,128)(2,1)}, f32[32,8,512]{2,1,0:T(8,128)}) custom-call(bf16[32,32,128]{2,1,0:T(8,128)(2,1)} %get-tuple-element.4.upd, f32[32,8,512]{2,1,0:T(8,128)} %bitcast.6), custom_call_target="tpu_custom_call" | custom-call | tf_op jit(solution)/shard_map/pallas_call | solution.py:618

commit v5 on v4

--- a/solution.py
+++ b/solution.py
@@ -28,7 +28,7 @@
 def kernel(
     grad, stats, steps, second, upd, moment,
     own, stat_v, second_v, moment_v,
-    r1, leaf, codes_out, codes_in, units_out, units_in, steps_v,
+    r1, leaf, codes_out, codes_in, units_out, units_in, sized, steps_v,
     outgoing, gathered, sums_out, sums_in, adam_pair, block, middle, back, roots,
     a_f, p_f, q_f, m_f, n_f,
     a_b, b_b, p_b, n_b, m_b,
@@ -60,15 +60,16 @@
     def hello(target):
         pl.semaphore_signal(barrier, inc=1, device_id={"fsdp": target}, device_id_type=MESH)
 
-    for turn in range(1, COLS):
-        hello(lax.rem(me + 2 * RINGS * turn, OWNERS))
-
-    def greet(t):
+    def greet(k):
+        t = RINGS + lax.div(k + 1, 2) * (1 - 2 * lax.rem(k, 2))
         low = lax.rem(me + t, 2 * RINGS)
         for high in range(COLS):
             hello(2 * RINGS * high + low)
 
-    each(2 * RINGS, greet, 1)
+    each(2 * RINGS - 1, greet)
+    for turn in range(1, COLS):
+        hello(lax.rem(me + 2 * RINGS * turn, OWNERS))
+
     own_copy = pltpu.make_async_copy(grad, own, local_sem.at[0])
     stat_copy = pltpu.make_async_copy(stats, stat_v, local_sem.at[1])
     second_copy = pltpu.make_async_copy(second, second_v, local_sem.at[2])
@@ -117,6 +118,8 @@
         index = 2 * batch + i
         return raw(way, 4 + index, 3, short_place(way, batch, i), leaf.at[way, index])
 
+    lane = lax.broadcasted_iota(jnp.int32, (1, 1, LANES), 2)
+
     def codes(way, index):
         return ring(
             way, codes_out.at[way, index], codes_in.at[way, index], code_send.at[way], sum_over_recv.at[way, index]
@@ -138,9 +141,10 @@
         parts = columns_of(value)
         size = [jnp.abs(part) for part in parts]
         largest = jnp.maximum(jnp.maximum(size[0], size[1]), jnp.maximum(size[2], size[3]))
+        largest = jnp.maximum(largest, pltpu.roll(largest, LANES // 2, 2))
         largest = jnp.maximum(jnp.max(largest, axis=1, keepdims=True), 1e-25)
         power = near_power(largest)
-        units_out[way, index] = power * 2.0**-14
+        units_out[way, index] = jnp.where(lane < LANES // 2, power[0:2], power[2:4]) * 2.0**-14
         units(way, index).start()
         inverse = near_power(2.0**14 / power)
         near = [(part * inverse + 1.5 * 2.0**23) - 1.5 * 2.0**23 for part in parts]
@@ -148,9 +152,12 @@
         codes(way, index).start()
 
     def received(way, index):
-        both = units_in.at[0, pl.ds(0, 17)]
-        pltpu.make_async_copy(both, both, sum_over_recv.at[way, index]).wait()
-        unit = units_in[way, index]
+        pltpu.make_async_copy(sized, sized, sum_over_recv.at[way, index]).wait()
+        here = jnp.broadcast_to(units_in[way, index], (2, ROWS, LANES))
+        there = pltpu.roll(here, LANES // 2, 2)
+        unit = jnp.concatenate(
+            [jnp.where(lane < LANES // 2, here, there), jnp.where(lane < LANES // 2, there, here)], axis=0
+        )
         parts = columns_of(codes_in[way, index].astype(jnp.int32).astype(F32))
         return jnp.concatenate([part * unit for part in parts], axis=2)
 
@@ -206,7 +213,8 @@
         sums_out[place] = jnp.sum(
             (squares[0] + squares[1]) + (squares[2] + squares[3]), axis=1, keepdims=True
         )
-        for index in range(COLS):
+        for turn in (2, 1, 3, 0):
+            index = lax.rem(x + turn, COLS)
             to_owner(
                 2 * (index * RINGS + col) + core,
                 outgoing.at[place, index],
@@ -257,11 +265,14 @@
     both_ways(1, short3)
     both_ways(1, long3)
     second_copy.wait()
-    each(4, finish)
+    def in_turn(k):
+        return 2 * lax.rem(k, 2) + lax.div(k, 2)
+
+    each(4, lambda k: finish(in_turn(k)))
     both_ways(1, short4)
     both_ways(1, long4)
-    each(FAR, finish, 4)
-    each(RINGS, finish_near, FAR)
+    each(FAR - 4, lambda k: finish(4 + in_turn(k)))
+    finish_near(FAR)
     moment_copy = pltpu.make_async_copy(moment_v, moment, local_sem.at[3])
     moment_copy.start()
 
@@ -291,7 +302,8 @@
             )
 
     each(RINGS, send_adam)
-    each(FAR, forward)
+    each(4, forward)
+    each(FAR - 4, lambda k: forward(4 + in_turn(k)))
 
     stat_copy.wait()
     for place in range(FAR, RINGS):
@@ -587,8 +599,9 @@
             pltpu.VMEM((2, 4) + chunk, BF16),
             pltpu.VMEM((2, 20) + chunk, jnp.int16),
             pltpu.VMEM((2, 20) + chunk, jnp.int16),
-            pltpu.VMEM((2, 20, COLS, 1, LANES), F32),
-            pltpu.VMEM((2, 20, COLS, 1, LANES), F32),
+            pltpu.VMEM((2, 20, 2, 1, LANES), F32),
+            pltpu.VMEM((2, 20, 2, 1, LANES), F32),
+            pltpu.VMEM((66, 1, LANES), F32),
             pltpu.SMEM((1,), jnp.int32),
             pltpu.VMEM((RINGS, COLS, 32, LANES), BF16),
             pltpu.VMEM((2, RINGS, COLS, 32, LANES), BF16),

time: 65.7 us -> 65 us (0.989)
  Pallas kernels: 64.2 us -> 63.5 us
    pallas_call x1, Pallas kernels: 62.2 us -> 61.5 us  [on_device(): pl.pallas_call(kernel, out_shape=(jax.ShapeDtypeStruct((HALF, 32, LANES),...]
where the time goes in v5:
time: 65 us; the launch traced here: 64.8 us
  Pallas kernels  63.5 us (98%)
  between operations  1.28 us (2%)
    pallas_call x1, Pallas kernels, on_device(): pl.pallas_call(kernel, out_shape=(jax.ShapeDtypeStruct((HALF, 32, LANES),...  61.5 us
    pallas_call x1, Pallas kernels, on_device(): pl.pallas_call(write_out, out_shape=(jax.ShapeDtypeStruct((HALF, ROWS, SI...  2 us

profile of v5, /device:TPU:1, one launch (start us, length us, event | category | flops | bytes accessed | tf_op | source)
XLA Modules:
  0.0 64.8 jit_solution(16121988755286913336)
XLA Ops:
  1.3 61.5 %shard_map.59 = (bf16[32,32,128]{2,1,0:T(8,128)(2,1)}, f32[4,8,8,512]{3,2,1,0:T(8,128)}) custom-call(bf16[8,4,8,8,512]{4,3,2,1,0:T(8,128)(2,1)} %bitcast.4, f32[512,512]{1,0:T(8,128)} %bitcast.5, s32[1]{0:T(128)S(6)} %copy.6.steps, f32[4,8,8,512]{3,2,1,0:T(8,128)} %bitcast.7), custom_call_target="tpu_custom_call" | custom-call | tf_op jit(solution)/shard_map/pallas_call | solution.py:585
  62.8 2.0 %shard_map.60 = (bf16[32,8,512]{2,1,0:T(8,128)(2,1)}, f32[32,8,512]{2,1,0:T(8,128)}) custom-call(bf16[32,32,128]{2,1,0:T(8,128)(2,1)} %get-tuple-element.4.upd, f32[32,8,512]{2,1,0:T(8,128)} %bitcast.6), custom_call_target="tpu_custom_call" | custom-call | tf_op jit(solution)/shard_map/pallas_call | solution.py:631
